TPU v7x, 768 devices: a whole 4x8x12 slice. The times are simulated.
768 devices in a mesh: space: 48 (over x, z_lo, core), dp: 16 (over z_hi, y).
Axes of the slice: x: 4, y: 8, z: 12 (z_hi: 2, z_lo: 6; z = z_hi * 6 + z_lo), core: 2. Of those that a mesh axis runs over, the one named last changes fastest.
Arguments:
- features: bfloat16 [32, 48, 72, 2048], P('dp', 'space'), may hold values from -6 to 6
- pointwise: bfloat16 [2, 2048, 256], P(None, 'dp'), may hold values from -0.125 to 0.125
- depthwise: bfloat16 [2, 9, 2048], P(None, None, 'dp'), may hold values from -2 to 2
- cotangent: bfloat16 [32, 48, 72, 512], P('dp', 'space'), may hold values from -6 to 6
Outputs:
- branches_out: bfloat16 [32, 48, 72, 512], P('dp', 'space')
- feature_grad: bfloat16 [32, 48, 72, 2048], P('dp', 'space')
- pointwise_grad: float32 [2, 2048, 256], P(None, 'dp')
- depthwise_grad: float32 [2, 9, 2048], P(None, None, 'dp')
All inputs are finite; a program needn't handle non-finite values.
Results may differ from a plain program's by a relative error of at most 0.014.
Values may be sent and summed in bfloat16 or wider, within the bound.
A program may use at most 32 MiB of HBM per device.

v0:
```python
import jax
import jax.numpy as jnp
from jax import lax
from jax.sharding import PartitionSpec as P

C = 2048
CO = 256
RATE_A = 12
RATE_B = 24


def shifted(value, axis, steps):
    count = lax.axis_size(axis)
    first, last = (max(0, -steps), min(count, count - steps))
    return lax.ppermute(value, axis, [(source, source + steps) for source in range(first, last)])


def column_tap(field, rate, side):
    width = field.shape[2]
    padded = jnp.pad(field, ((0, 0), (0, 0), (rate, rate), (0, 0)))
    start = rate + side * rate
    return padded[:, :, start : start + width, :]


def row_taps(field, offset):
    return shifted(field, "space", offset)


def grad_taps(field, offset):
    return shifted(field, "space", offset)


def transposed(left, weight):
    return lax.dot_general(
        left, weight, (((1,), (1,)), ((), ())), preferred_element_type=jnp.float32
    )


def body(features, pointwise, depthwise, cotangent):
    img_count = features.shape[0]
    rows_dev = features.shape[1]
    width = features.shape[2]
    w_full, k_full = (
        lax.all_gather(pointwise, "dp", axis=1, tiled=True),
        lax.all_gather(depthwise, "dp", axis=2, tiled=True),
    )
    outputs = []
    grad_total = jnp.zeros(features.shape, jnp.float32)
    w_parts = []
    k_parts = []
    for branch, rate in enumerate((RATE_A, RATE_B)):
        offset = rate // rows_dev
        rows_near = {-1: row_taps(features, offset), 0: features, 1: row_taps(features, -offset)}
        dsum = jnp.zeros(features.shape, jnp.float32)
        for up in (-1, 0, 1):
            for side in (-1, 0, 1):
                tap = (up + 1) * 3 + (side + 1)
                dsum = dsum + column_tap(rows_near[up], rate, side).astype(jnp.float32) * k_full[
                    branch, tap
                ].astype(jnp.float32)
        dconv = dsum.astype(jnp.bfloat16)
        flat = dconv.reshape(-1, C)
        weight = w_full[branch]
        pre = jnp.dot(flat, weight, preferred_element_type=jnp.float32)
        sig = jax.nn.sigmoid(pre)
        outputs.append((pre * sig).reshape(img_count, rows_dev, width, CO).astype(jnp.bfloat16))
        cot_part = (
            cotangent[..., branch * CO : (branch + 1) * CO].reshape(-1, CO).astype(jnp.float32)
        )
        gpre = (cot_part * sig * (1.0 + pre * (1.0 - sig))).astype(jnp.bfloat16)
        gdconv = transposed(gpre, weight).astype(jnp.bfloat16).reshape(features.shape)
        w_parts.append(
            lax.dot_general(
                flat, gpre, (((0,), (0,)), ((), ())), preferred_element_type=jnp.float32
            )
        )
        gd_wide = gdconv.astype(jnp.float32)
        tap_rows = []
        for up in (-1, 0, 1):
            for side in (-1, 0, 1):
                source = column_tap(rows_near[up], rate, side).astype(jnp.float32)
                tap_rows.append(jnp.sum(source * gd_wide, axis=(0, 1, 2)))
        k_parts.append(jnp.stack(tap_rows))
        grad_near = {1: grad_taps(gdconv, offset), 0: gdconv, -1: grad_taps(gdconv, -offset)}
        for up in (-1, 0, 1):
            for side in (-1, 0, 1):
                tap = (up + 1) * 3 + (side + 1)
                grad_total = grad_total + column_tap(grad_near[up], rate, -side).astype(
                    jnp.float32
                ) * k_full[branch, tap].astype(jnp.float32)
    part_w = jnp.stack(w_parts)
    part_k = jnp.stack(k_parts)
    shard_w, shard_k = (
        lax.psum_scatter(part_w.astype(jnp.bfloat16), "dp", scatter_dimension=1, tiled=True).astype(
            jnp.float32
        ),
        lax.psum_scatter(part_k.astype(jnp.bfloat16), "dp", scatter_dimension=2, tiled=True).astype(
            jnp.float32
        ),
    )
    sum_w, sum_k = lax.psum((shard_w, shard_k), "space")
    cells = lax.axis_size("dp") * img_count * lax.axis_size("space") * rows_dev * width
    factor = 1.0 / jnp.sqrt(jnp.float32(cells))
    branches_out = jnp.concatenate(outputs, axis=-1)
    return (branches_out, grad_total.astype(jnp.bfloat16), sum_w * factor, sum_k * factor)


def solution(mesh):
    return jax.shard_map(
        body,
        mesh=mesh,
        in_specs=(
            P("dp", "space", None, None),
            P(None, "dp", None),
            P(None, None, "dp"),
            P("dp", "space", None, None),
        ),
        out_specs=(
            P("dp", "space", None, None),
            P("dp", "space", None, None),
            P(None, "dp", None),
            P(None, None, "dp"),
        ),
        check_vma=False,
    )
```

profile of v0, /device:TPU:57, one launch (start us, length us, event | category | flops | bytes accessed | tf_op | source)
XLA Modules:
  0.0 907.5 jit_solution(2198469458865513237)
XLA Ops:
  7.2 0.0 all-gather.2.cloned.1.call-start
  7.2 0.7 all-gather.2.cloned.1.call-update
  7.9 0.0 reduce-scatter.7.cloned.1.call-start
  8.0 3.2 collective-permute-start
  11.1 1.3 collective-permute-start.1
  12.4 5.5 collective-permute-start.2
  17.9 1.3 collective-permute-start.3
  19.2 52.7 %all_gather.6 = bf16[2,9,2048]{2,0,1:T(2,128)(2,1)S(1)} all-gather(bf16[2,9,128]{2,0,1:T(2,128)(2,1)} %param.6), channel_id=1, replica_groups=mesh['space'=48,'dp'=16] {'dp'}, dimensions={2}, use_global_device_ids=true | all-gather | bytes 78336 | tf_op jit(solution)/shard_map/all_gather | solution.py:45
  72.0 0.1 slice_convert_fusion.17
  72.2 0.0 copy-start.10
  72.2 0.9 fusion.59
  73.2 1.1 fusion.10
  74.6 0.7 copy-done.5
  75.3 0.2 copy-done.7
  75.5 0.8 fusion.19
  76.3 63.0 %all-gather.2.cloned.1.call-done = bf16[2,2048,256]{2,1,0:T(8,128)(2,1)} async-done(((bf16[2,128,256]{2,1,0:T(8,128)(2,1)}), bf16[2,2048,256]{2,1,0:T(8,128)(2,1)}) %all-gather.2.cloned.1.call-update) | async-done | bytes 2097168 | tf_op jit(solution)/shard_map/all_gather | solution.py:44
  139.3 2.4 fusion.58
  141.6 0.5 fusion
  142.2 1.0 fusion.56
  143.2 1.5 fusion.1
  144.7 0.5 convolution_convert_fusion.3
  145.2 0.5 convolution_convert_fusion.2
  145.7 0.1 copy-done.6
  145.7 0.2 copy-done.8
  145.9 0.4 copy-done.2
  146.3 0.2 copy-done.4
  146.5 2.8 fusion.42
  149.6 0.1 stack.116
  149.7 0.1 stack.127
  149.9 0.8 copy.40
  150.8 1.3 reshape.284
  152.0 0.0 reduce-scatter.7.cloned.1.call-update
  152.1 0.0 reduce-scatter.5.cloned.1.call-start
  152.1 2.8 pad_maximum_fusion
  154.9 0.0 reduce-scatter.5.cloned.1.call-update
  154.9 1.3 collective-permute-start.4
  156.2 4.0 collective-permute-start.5
  160.2 1.3 collective-permute-start.6
  161.5 5.6 collective-permute-start.7
  167.1 1.6 pad_maximum_fusion.1
  168.7 210.9 %reduce-scatter.7.cloned.1.call-done = bf16[128,18]{1,0:T(8,128)(2,1)} async-done(((bf16[2048,18]{1,0:T(8,128)(2,1)}), bf16[128,18]{1,0:T(8,128)(2,1)}) %reduce-scatter.7.cloned.1.call-update) | async-done | bytes 4624
  379.6 1.5 reshape.285
  381.1 1.5 copy.41
  382.6 4.0 fusion.52
  386.7 242.7 %reduce-scatter.5.cloned.1.call-done = bf16[2,128,256]{2,1,0:T(8,128)(2,1)} async-done(((bf16[2,2048,256]{2,1,0:T(8,128)(2,1)}), bf16[2,128,256]{2,1,0:T(8,128)(2,1)}) %reduce-scatter.5.cloned.1.call-update) | async-done | bytes 131088 | tf_op jit(solution)/shard_map/reduce_scatter | solution.py:94
  629.3 270.3 %all-reduce.14 = (f32[2,128,256]{2,1,0:T(8,128)S(1)}, f32[2,9,128]{2,1,0:T(8,128)S(1)}) all-reduce(bf16[2,128,256]{2,1,0:T(8,128)(2,1)} %reduce-scatter.5.cloned.1.call-done, bf16[2,9,128]{2,1,0:T(8,128)(2,1)} %copy.41), channel_id=1, replica_groups=mesh['space'=48,'dp'=16] {'space'}, use_global_device_ids=true, to_apply=%region_1.2 | all-reduce | flops 67840 | bytes 407040 | tf_op jit(solution)/shard_map/psum | solution.py:101
  899.6 0.7 broadcast_multiply_fusion
  900.4 0.6 copy.39
  (73 shorter events, 0.3 us)
Async XLA Ops:
  7.2 66.1 %copy-start = (bf16[2,1,72,2048]{3,2,1,0:T(8,128)(2,1)S(1)}, bf16[2,1,72,2048]{3,2,1,0:T(8,128)(2,1)}, u32[]{:S(2)}) copy-start(bf16[2,1,72,2048]{3,2,1,0:T(8,128)(2,1)} %param.4) | copy-start | bytes 1769476
  7.2 132.1 %all-gather.2.cloned.1.call-start = ((), (), s32[]{:S(2)}) async-start(), calls=%async_computation.2 | async-start | bytes 2228224 | tf_op jit(solution)/shard_map/all_gather | solution.py:44
  7.9 371.7 %reduce-scatter.7.cloned.1.call-start = ((), (), s32[]{:S(2)}) async-start(), calls=%async_computation.4 | async-start | bytes 557056
  8.0 65.2 %collective-permute-start = (bf16[2,1,72,2048]{3,2,1,0:T(8,128)(2,1)}, bf16[2,1,72,2048]{3,2,1,0:T(8,128)(2,1)S(1)}, u32[]{:S(2)}, u32[]{:S(2)}) collective-permute-start(bf16[2,1,72,2048]{3,2,1,0:T(8,128)(2,1)} %param.4), channel_id=1, source_target_pairs={{0,192},{16,208},{32,224},{48,240},{64,256},{80,272},{96,288},{112... | collective-permute-start | bytes 1769480 | tf_op jit(solution)/shard_map/ppermute | solution.py:15
  11.1 62.1 %collective-permute-start.1 = (bf16[2,1,72,2048]{3,2,1,0:T(8,128)(2,1)}, bf16[2,1,72,2048]{3,2,1,0:T(8,128)(2,1)S(1)}, u32[]{:S(2)}, u32[]{:S(2)}) collective-permute-start(bf16[2,1,72,2048]{3,2,1,0:T(8,128)(2,1)} %param.4), channel_id=1, source_target_pairs={{192,0},{208,16},{224,32},{240,48},{256,64},{272,80},{288,96},{304... | collective-permute-start | bytes 1769480 | tf_op jit(solution)/shard_map/ppermute | solution.py:15
  12.4 62.0 %collective-permute-start.2 = (bf16[2,1,72,2048]{3,2,1,0:T(8,128)(2,1)}, bf16[2,1,72,2048]{3,2,1,0:T(8,128)(2,1)S(1)}, u32[]{:S(2)}, u32[]{:S(2)}) collective-permute-start(bf16[2,1,72,2048]{3,2,1,0:T(8,128)(2,1)} %param.4), channel_id=1, source_target_pairs={{0,384},{16,400},{32,416},{48,432},{64,448},{80,464},{96,480},{112... | collective-permute-start | bytes 1769480 | tf_op jit(solution)/shard_map/ppermute | solution.py:15
  17.9 56.5 %collective-permute-start.3 = (bf16[2,1,72,2048]{3,2,1,0:T(8,128)(2,1)}, bf16[2,1,72,2048]{3,2,1,0:T(8,128)(2,1)S(1)}, u32[]{:S(2)}, u32[]{:S(2)}) collective-permute-start(bf16[2,1,72,2048]{3,2,1,0:T(8,128)(2,1)} %param.4), channel_id=1, source_target_pairs={{384,0},{400,16},{416,32},{432,48},{448,64},{464,80},{480,96},{496... | collective-permute-start | bytes 1769480 | tf_op jit(solution)/shard_map/ppermute | solution.py:15
  72.1 2.3 copy-start.18
  72.1 2.3 copy-start.19
  72.1 2.3 copy-start.20
  72.1 2.3 copy-start.21
  72.1 2.3 copy-start.22
  72.1 2.3 copy-start.23
  72.1 2.3 copy-start.24
  72.1 2.3 copy-start.25
  72.2 2.3 copy-start.10
  72.2 2.3 copy-start.11
  72.2 2.3 copy-start.12
  72.2 2.3 copy-start.13
  72.2 2.3 copy-start.14
  72.2 2.3 copy-start.15
  72.2 2.3 copy-start.16
  72.2 2.3 copy-start.17
  73.2 1.2 copy-start.1
  73.2 1.2 copy-start.3
  74.5 0.8 copy-start.5
  74.5 1.0 copy-start.7
  139.3 2.9 copy-start.9
  144.6 1.1 copy-start.6
  144.7 1.2 copy-start.8
  145.1 1.2 copy-start.2
  145.2 1.3 copy-start.4
  152.1 477.3 %reduce-scatter.5.cloned.1.call-start = ((), (), s32[]{:S(2)}) async-start(), calls=%async_computation.3 | async-start | bytes 2228224 | tf_op jit(solution)/shard_map/reduce_scatter | solution.py:94
  154.9 227.7 %collective-permute-start.4 = (bf16[2,1,72,2048]{3,2,1,0:T(8,128)(2,1)S(1)}, bf16[2,1,72,2048]{3,2,1,0:T(8,128)(2,1)S(1)}, u32[]{:S(2)}, u32[]{:S(2)}) collective-permute-start(bf16[2,1,72,2048]{3,2,1,0:T(8,128)(2,1)S(1)} %bitcast.73), channel_id=1, source_target_pairs={{192,0},{208,16},{224,32},{240,48},{256,64},{272,80},{288,96},{304... | collective-permute-start | bytes 1769480 | tf_op jit(solution)/shard_map/ppermute | solution.py:15
  156.2 226.4 %collective-permute-start.5 = (bf16[2,1,72,2048]{3,2,1,0:T(8,128)(2,1)S(1)}, bf16[2,1,72,2048]{3,2,1,0:T(8,128)(2,1)S(1)}, u32[]{:S(2)}, u32[]{:S(2)}) collective-permute-start(bf16[2,1,72,2048]{3,2,1,0:T(8,128)(2,1)S(1)} %bitcast.74), channel_id=1, source_target_pairs={{0,192},{16,208},{32,224},{48,240},{64,256},{80,272},{96,288},{112... | collective-permute-start | bytes 1769480 | tf_op jit(solution)/shard_map/ppermute | solution.py:15
  160.2 222.4 %collective-permute-start.6 = (bf16[2,1,72,2048]{3,2,1,0:T(8,128)(2,1)S(1)}, bf16[2,1,72,2048]{3,2,1,0:T(8,128)(2,1)S(1)}, u32[]{:S(2)}, u32[]{:S(2)}) collective-permute-start(bf16[2,1,72,2048]{3,2,1,0:T(8,128)(2,1)S(1)} %bitcast.77), channel_id=1, source_target_pairs={{384,0},{400,16},{416,32},{432,48},{448,64},{464,80},{480,96},{496... | collective-permute-start | bytes 1769480 | tf_op jit(solution)/shard_map/ppermute | solution.py:15
  161.5 221.1 %collective-permute-start.7 = (bf16[2,1,72,2048]{3,2,1,0:T(8,128)(2,1)S(1)}, bf16[2,1,72,2048]{3,2,1,0:T(8,128)(2,1)S(1)}, u32[]{:S(2)}, u32[]{:S(2)}) collective-permute-start(bf16[2,1,72,2048]{3,2,1,0:T(8,128)(2,1)S(1)} %bitcast.78), channel_id=1, source_target_pairs={{0,384},{16,400},{32,416},{48,432},{64,448},{80,464},{96,480},{112... | collective-permute-start | bytes 1769480 | tf_op jit(solution)/shard_map/ppermute | solution.py:15
Sparse Core Ops, SparseCore 0:
  11.7 127.4 all-gather.1
  152.2 227.3 reduce-scatter.6
  385.5 243.7 reduce-scatter.4
where the time goes:
time: 918 us; the launch traced here: 908 us
  waiting for transfers between devices  517 us (56%)
  blocking collectives  323 us (35%)
  starting transfers between devices  23.5 us (3%)
  between operations  14.4 us (2%)
  other arithmetic  14 us (2%)
    psum x1, blocking collectives, body(): sum_w, sum_k = lax.psum((shard_w, shard_k), 'space')  270 us
    reduce_scatter x1, waiting for transfers between devices, body(): lax.psum_scatter(part_w.astype(jnp.bfloat16), 'dp', scatter_dimension=1,...  243 us
    unnamed x4, waiting for transfers between devices  212 us
    all_gather x1, waiting for transfers between devices, body(): lax.all_gather(pointwise, 'dp', axis=1, tiled=True)  63 us
    all_gather x1, blocking collectives, body(): lax.all_gather(depthwise, 'dp', axis=2, tiled=True)  52.7 us
    ppermute x8, starting transfers between devices, shifted(): lax.ppermute(value, axis, [(source, source + steps) for source in range(f...  23.4 us
  transfers between devices with their start and end apart: 11, of which 3 were waited for; matrix products, arithmetic and copies ran while one was open for 2% of the time, Pallas kernels for 0%

commit v1 on v0

v1 whole, which is shorter than its diff:
```python
import jax
import jax.numpy as jnp
from jax import lax
from jax.experimental import pallas as pl
from jax.experimental.pallas import tpu as pltpu
from jax.sharding import PartitionSpec as P

C = 2048
CO = 256
CELLS = 144
LANES = 128
PART = 512
BF16 = jnp.bfloat16
F32 = jnp.float32
MESH = pl.DeviceIdType.MESH
FACTOR = 1.0 / (110592.0**0.5)


def device_at(x, z_low, core, z_high, y):
    return {"space": (x * 6 + z_low) * 2 + core, "dp": z_high * 8 + y}


def local_wait(ref, sem):
    pltpu.make_async_copy(ref, ref, sem).wait()


def kernel(
    feat, pw, kin, cot,
    out, fgrad, pgrad, kgrad,
    rows, wide, moved, taps, dcv, wts, away_w, away_k,
    own_pre, send_pre, got_pre, gpre, ga, ga_moved, gb, fg_send,
    wg_wide, wg, wg_core, wg_y, wg_y_got, wg_z, wg_z_got, wg_red,
    kg, kg_core, kg_y, kg_y_got, kg_z, kg_z_got, kg_red, fin, kfin,
    f_send, f_recv, own_sem, a_send, a_recv, w_send, w_recv, k_send, k_recv, wc_send, wc_recv,
    p_send, p_recv, g_send, g_recv, o_send, o_recv,
    c_send, c_recv, y_send, y_recv, z_send, z_recv, b_send, b_recv, e_send, e_recv,
    kc_send, kc_recv, ky_send, ky_recv, kz_send, kz_recv, kb_send, kb_recv, ke_send, ke_recv,
):
    space = lax.axis_index("space")
    dp = lax.axis_index("dp")
    x = space // 12
    zl = (space // 2) % 6
    core = space % 2
    zh = dp // 8
    y = dp % 8
    z = zh * 6 + zl
    plane = y // 2
    at_home = x == plane
    mate = device_at(x, zl, 1 - core, zh, y)
    sent = []

    def remote(src, dst, send_sem, recv_sem, target):
        return pltpu.make_async_remote_copy(
            src_ref=src, dst_ref=dst, send_sem=send_sem, recv_sem=recv_sem,
            device_id=target, device_id_type=MESH,
        )

    def send(src, dst, send_sem, recv_sem, target):
        copy = remote(src, dst, send_sem, recv_sem, target)
        copy.start()
        sent.append((None, copy))

    def send_if(cond, src, dst, send_sem, recv_sem, target):
        copy = remote(src, dst, send_sem, recv_sem, target)
        here = pltpu.make_async_copy(src, dst, recv_sem)

        @pl.when(cond)
        def _():
            copy.start()

        @pl.when(jnp.logical_not(cond))
        def _():
            here.start()

        sent.append((cond, copy))

    def x_peer(k):
        return device_at((x + k) % 4, zl, core, zh, y)

    def z_peer(k):
        other = (z + k) % 12
        return device_at(x, other % 6, core, other // 6, y)

    sides = (slice(0, 256), slice(256, 512))

    def channels(of_x, side):
        return pl.ds(pl.multiple_of(side * 1024 + of_x * 256, 256), 256)

    barrier = pltpu.get_barrier_semaphore()

    def greet(target):
        pl.semaphore_signal(barrier, inc=1, device_id=target, device_id_type=MESH)

    count = 0
    for k in (1, 3, 2):
        greet(x_peer(k))
        count += 1
    greet(mate)
    count += 1
    for k in range(1, 12):
        greet(z_peer(k))
        count += 1
    for k in range(1, 8):
        greet(device_at(plane, zl, core, zh, (y + k) % 8))
        count += 1
    for other in range(4):
        for near in range(2):
            target_y = 2 * x + near
            same = jnp.logical_and(other == x, target_y == y)

            @pl.when(jnp.logical_not(same))
            def _(other=other, target_y=target_y):
                greet(device_at(other, zl, core, zh, target_y))

    @pl.when(jnp.logical_not(at_home))
    def _():
        greet(device_at(plane, zl, core, zh, y))

    count += 9
    moved[...] = jnp.zeros_like(moved)
    ga_moved[...] = jnp.zeros_like(ga_moved)
    kg[...] = jnp.zeros_like(kg)
    pl.semaphore_wait(barrier, count - 2 * at_home.astype(jnp.int32))

    for k in (2, 1, 3):
        for side in range(2):
            send(
                feat.at[:, channels((x + k) % 4, side)], rows.at[x, :, sides[side]],
                f_send.at[side, k], f_recv.at[side, k], x_peer(k),
            )
    own_rows = [
        pltpu.make_async_copy(
            feat.at[:, channels(x, side)], rows.at[x, :, sides[side]], own_sem.at[side]
        )
        for side in range(2)
    ]
    for copy in own_rows:
        copy.start()

    piece = pl.ds(pl.multiple_of(core * 64 + x * 16, 16), 16)
    antipode = device_at(x, zl, core, 1 - zh, y)
    send(kin, away_k, a_send.at[0], a_recv.at[0], antipode)
    send(pw.at[:, piece, :], away_w, a_send.at[1], a_recv.at[1], antipode)
    near_slot = zh * 2 + y % 2
    far_slot = (1 - zh) * 2 + y % 2
    not_home = jnp.logical_not(at_home)

    def spread_taps(src, slot, base):
        for k in range(8):
            target = device_at(plane, zl, core, zh, (y + k) % 8)
            if k == 0:
                here = pltpu.make_async_copy(src, taps.at[slot], k_recv.at[slot])

                @pl.when(at_home)
                def _(here=here):
                    here.start()
            else:
                copy = remote(src, taps.at[slot], k_send.at[base + k], k_recv.at[slot], target)

                @pl.when(at_home)
                def _(copy=copy):
                    copy.start()

                sent.append((at_home, copy))

    def spread_weights(src, slot, base):
        for k in range(8):
            target = device_at(plane, zl, core, zh, (y + k) % 8)
            dst = wts.at[:, slot, core, pl.ds(pl.multiple_of(x * 16, 16), 16)]
            if k == 0:
                send_if(not_home, src, dst, w_send.at[base], w_recv, target)
            else:
                send(src, dst, w_send.at[base + k], w_recv, target)

    spread_taps(kin, near_slot, 0)
    spread_weights(pw.at[:, piece, :], near_slot, 0)
    remote(kin, away_k, a_send.at[0], a_recv.at[0], antipode).wait_recv()
    spread_taps(away_k, far_slot, 8)
    remote(pw.at[:, piece, :], away_w, a_send.at[1], a_recv.at[1], antipode).wait_recv()
    spread_weights(away_w, far_slot, 8)

    for copy in own_rows:
        copy.wait()
    for k in (1, 3, 2):
        for side in range(2):
            remote(
                rows.at[x, :, sides[side]], rows.at[(x - k + 4) % 4, :, sides[side]],
                f_send.at[side, k], f_recv.at[side, k], x_peer(k),
            ).wait_recv()
    for slot in range(4):
        local_wait(taps.at[slot], k_recv.at[slot])

    def stencils(tile):
        lanes = pl.ds(pl.multiple_of(tile * LANES, LANES), LANES)
        for r in range(4):
            value = rows[r, :, lanes].astype(F32)
            wide[r, :, lanes] = value
            for i in range(2):
                moved[r, i, 20:92, lanes] = value[72 * i : 72 * i + 72]
        weights = taps[tile].astype(F32)

        def tap(b, u, v):
            t = (u + 1) * 3 + v + 1
            return weights[b, t : t + 1]

        for r in range(4):
            pieces = []
            for i in range(2):
                for q in range(3):
                    total = None
                    for u in (-1, 0, 1):
                        if not 0 <= r + u < 4:
                            continue
                        term = (
                            tap(0, u, 0) * wide[r + u, 72 * i + 24 * q : 72 * i + 24 * q + 24, lanes]
                            + tap(0, u, -1) * moved[r + u, i, 24 * q + 8 : 24 * q + 32, lanes]
                            + tap(0, u, 1) * moved[r + u, i, 24 * q + 32 : 24 * q + 56, lanes]
                        )
                        total = term if total is None else total + term
                    pieces.append(total)
            dcv[0, r, :, lanes] = jnp.concatenate(pieces, axis=0).astype(BF16)
            pieces = []
            for i in range(2):
                for q in range(3):
                    total = None
                    for u in (-1, 0, 1):
                        if not 0 <= r + 2 * u < 4:
                            continue
                        for v in (-1, 0, 1):
                            if not 0 <= q + v < 3:
                                continue
                            start = 72 * i + 24 * (q + v)
                            term = tap(1, u, v) * wide[r + 2 * u, start : start + 24, lanes]
                            total = term if total is None else total + term
                    pieces.append(total)
            dcv[1, r, :, lanes] = jnp.concatenate(pieces, axis=0).astype(BF16)

    pl.loop(0, 2)(stencils)
    local_wait(wts.at[:, :, core], w_recv)
    send(wts.at[:, :, core], wts.at[:, :, core], wc_send, wc_recv, mate)
    pl.loop(2, 4)(stencils)
    remote(
        wts.at[:, :, core], wts.at[:, :, 1 - core], wc_send, wc_recv, mate
    ).wait_recv()

    for k in (2, 1, 3, 0):
        r = (x + k) % 4
        for b in range(2):
            part = jnp.dot(
                dcv[b, r], wts[b].reshape(PART, CO), preferred_element_type=F32
            )
            if k:
                send_pre[k, :, b * CO : (b + 1) * CO] = part.astype(BF16)
            else:
                own_pre[:, b * CO : (b + 1) * CO] = part
        if k:
            send(send_pre.at[k], got_pre.at[k], p_send.at[k], p_recv.at[k], x_peer(k))
    for k in (1, 3, 2):
        remote(send_pre.at[k], got_pre.at[k], p_send.at[k], p_recv.at[k], x_peer(k)).wait_recv()
    for b in range(2):
        cols = slice(b * CO, (b + 1) * CO)
        pre = own_pre[:, cols]
        for k in (1, 3, 2):
            pre = pre + got_pre[k, :, cols].astype(F32)
        sig = 1.0 / (1.0 + jnp.exp(-pre))
        gpre[x, :, cols] = (
            cot[:, cols].astype(F32) * sig * (1.0 + pre * (1.0 - sig))
        ).astype(BF16)
        out[:, cols] = (pre * sig).astype(BF16)
    for k in (2, 1, 3):
        send(gpre.at[x], gpre.at[x], g_send.at[k], g_recv.at[k], x_peer(k))
    for k in (1, 3, 2):
        remote(
            gpre.at[x], gpre.at[(x - k + 4) % 4], g_send.at[k], g_recv.at[k], x_peer(k)
        ).wait_recv()

    @pl.loop(0, 4)
    def _(tile):
        lanes = pl.ds(pl.multiple_of(tile * LANES, LANES), LANES)
        for b in range(2):
            grad = lax.dot_general(
                dcv[b, :, :, lanes].reshape(4 * CELLS, LANES),
                gpre[:, :, b * CO : (b + 1) * CO].reshape(4 * CELLS, CO),
                (((0,), (0,)), ((), ())),
                preferred_element_type=F32,
            )
            for half in range(2):
                block = grad[64 * half : 64 * half + 64]
                wg_wide[half, tile, b] = block
                wg[half, tile, b] = block.astype(BF16)

    send(wg.at[1 - core], wg_core, c_send, c_recv, mate)

    @pl.loop(0, 4)
    def _(r):
        for b in range(2):
            back = lax.dot_general(
                gpre[r, :, b * CO : (b + 1) * CO],
                wts[b].reshape(PART, CO),
                (((1,), (1,)), ((), ())),
                preferred_element_type=F32,
            )
            if b:
                gb[r] = back
            else:
                ga[r] = back
                for i in range(2):
                    ga_moved[r, i, 20:92] = back[72 * i : 72 * i + 72]

    remote(wg.at[1 - core], wg_core, c_send, c_recv, mate).wait_recv()
    for k in range(8):
        to = (y + k) % 8
        slot = to // 2
        part = pl.ds(pl.multiple_of((to % 2) * 32, 32), 32)
        for b in range(2):
            wg_y[k, b] = (
                wg_wide[core, slot, b, part] + wg_core[slot, b, part].astype(F32)
            ).astype(BF16)
        if k:
            send(
                wg_y.at[k], wg_y_got.at[k], y_send.at[k], y_recv.at[k],
                device_at(x, zl, core, zh, to),
            )

    @pl.loop(0, 4)
    def _(tile):
        lanes = pl.ds(pl.multiple_of(tile * LANES, LANES), LANES)
        for b in range(2):
            step = b + 1
            for u in (-1, 0, 1):
                sums = [None, None, None]
                for r in range(4):
                    if not 0 <= r + step * u < 4:
                        continue
                    for i in range(2):
                        for q in range(3):
                            start = 72 * i + 24 * q
                            if b:
                                grad = gb[r, start : start + 24, lanes]
                            else:
                                grad = ga[r, start : start + 24, lanes]
                            for v in (-1, 0, 1):
                                if b:
                                    if not 0 <= q + v < 3:
                                        continue
                                    source = wide[r + 2 * u, start + 24 * v : start + 24 * v + 24, lanes]
                                elif v == 0:
                                    source = wide[r + u, start : start + 24, lanes]
                                else:
                                    begin = 24 * q + 20 + 12 * v
                                    source = moved[r + u, i, begin : begin + 24, lanes]
                                term = source * grad
                                term = term[0:8] + term[8:16] + term[16:24]
                                old = sums[v + 1]
                                sums[v + 1] = term if old is None else old + term
                for v in (-1, 0, 1):
                    t = (u + 1) * 3 + v + 1
                    total = jnp.sum(sums[v + 1], axis=0, keepdims=True)
                    kg[t // 8, tile, b, t % 8 : t % 8 + 1] = total

    send(kg.at[1 - core], kg_core, kc_send, kc_recv, mate)

    def gradient(tile):
        lanes = pl.ds(pl.multiple_of(tile * LANES, LANES), LANES)
        weights = taps[tile].astype(F32)

        def tap(b, u, v):
            t = (u + 1) * 3 + v + 1
            return weights[b, t : t + 1]

        for r in range(4):
            pieces = []
            for i in range(2):
                for q in range(3):
                    total = None
                    start = 72 * i + 24 * q
                    for u in (-1, 0, 1):
                        if 0 <= r - u < 4:
                            term = (
                                tap(0, u, 0) * ga[r - u, start : start + 24, lanes]
                                + tap(0, u, 1) * ga_moved[r - u, i, 24 * q + 8 : 24 * q + 32, lanes]
                                + tap(0, u, -1) * ga_moved[r - u, i, 24 * q + 32 : 24 * q + 56, lanes]
                            )
                            total = term if total is None else total + term
                        if 0 <= r - 2 * u < 4:
                            for v in (-1, 0, 1):
                                if 0 <= q - v < 3:
                                    begin = start - 24 * v
                                    term = tap(1, u, v) * gb[r - 2 * u, begin : begin + 24, lanes]
                                    total = term if total is None else total + term
                    pieces.append(total)
            fg_send[r, :, lanes] = jnp.concatenate(pieces, axis=0).astype(BF16)

    pl.loop(0, 2)(gradient)
    remote(kg.at[1 - core], kg_core, kc_send, kc_recv, mate).wait_recv()
    for k in range(8):
        to = (y + k) % 8
        kg_y[k] = kg[core, to // 2, to % 2] + kg_core[to // 2, to % 2]
        if k:
            send(
                kg_y.at[k], kg_y_got.at[k], ky_send.at[k], ky_recv.at[k],
                device_at(x, zl, core, zh, to),
            )
    pl.loop(2, 4)(gradient)
    for k in (2, 1, 3):
        for side in range(2):
            send(
                fg_send.at[(x + k) % 4, :, sides[side]], fgrad.at[:, channels(x, side)],
                o_send.at[side, k], o_recv.at[side, k], x_peer(k),
            )
    own_grad = [
        pltpu.make_async_copy(
            fg_send.at[x, :, sides[side]], fgrad.at[:, channels(x, side)], own_sem.at[side]
        )
        for side in range(2)
    ]
    for copy in own_grad:
        copy.start()

    for k in range(1, 8):
        remote(
            wg_y.at[k], wg_y_got.at[k], y_send.at[k], y_recv.at[k], mate
        ).wait_recv()
    for b in range(2):
        total = wg_y[0, b].astype(F32)
        for k in range(1, 8):
            total = total + wg_y_got[k, b].astype(F32)
        for h in range(2):
            for lane in range(2):
                wg_z[b * 4 + h * 2 + lane] = total[
                    16 * h : 16 * h + 16, 128 * lane : 128 * lane + 128
                ].astype(BF16)
    for j in range(8):
        owner = j if j < 4 else j + 2
        send_if(
            z != owner, wg_z.at[j], wg_z_got.at[z], z_send.at[j], z_recv,
            device_at(x, owner % 6, core, owner // 6, y),
        )
    for k in range(1, 8):
        remote(
            kg_y.at[k], kg_y_got.at[k], ky_send.at[k], ky_recv.at[k], mate
        ).wait_recv()
    total = kg_y[0]
    for k in range(1, 8):
        total = total + kg_y_got[k]
    kg_z[...] = total
    send_if(
        z != 4, kg_z, kg_z_got.at[z], kz_send, kz_recv, device_at(x, 4, core, 0, y)
    )

    half = y % 2
    home_z = y // 4
    home_y = 2 * x + (y // 2) % 2
    back_sent = []

    def spread_sums(src, dst, send_sems, recv_sem):
        for n in range(24):
            to_x, to_z = n // 6, n % 6
            same = (to_x == x) & (to_z == zl) & (home_z == zh) & (home_y == y)
            copy = remote(
                src, dst, send_sems.at[n], recv_sem, device_at(to_x, to_z, core, home_z, home_y)
            )
            here = pltpu.make_async_copy(src, dst, recv_sem)

            @pl.when(jnp.logical_not(same))
            def _(copy=copy):
                copy.start()

            @pl.when(same)
            def _(here=here):
                here.start()

            back_sent.append((same, copy))

    def wait_sums():
        for same, copy in back_sent:

            @pl.when(jnp.logical_not(same))
            def _(copy=copy):
                copy.wait_send()

        back_sent.clear()

    @pl.when(zl < 4)
    def _():
        local_wait(wg_z_got, z_recv)
        total = wg_z_got[0].astype(F32)
        for n in range(1, 12):
            total = total + wg_z_got[n].astype(F32)
        wg_red[...] = (total * FACTOR).astype(BF16)
        spread_sums(wg_red, fin.at[core, half, zh * 4 + zl], b_send, b_recv)
        wait_sums()

    @pl.when(z == 4)
    def _():
        local_wait(kg_z_got, kz_recv)
        total = kg_z_got[0]
        for n in range(1, 12):
            total = total + kg_z_got[n]
        kg_red[...] = total * FACTOR
        spread_sums(kg_red, kfin.at[core, half], kb_send, kb_recv)
        wait_sums()

    local_wait(fin.at[core], b_recv)
    send(fin.at[core], fin.at[core], e_send, e_recv, mate)
    local_wait(kfin.at[core], kb_recv)
    send(kfin.at[core], kfin.at[core], ke_send, ke_recv, mate)
    remote(fin.at[core], fin.at[1 - core], e_send, e_recv, mate).wait_recv()
    remote(kfin.at[core], kfin.at[1 - core], ke_send, ke_recv, mate).wait_recv()
    for c in range(2):
        for h in range(2):
            for j in range(8):
                b, h2, lane = j // 4, (j // 2) % 2, j % 2
                first = 64 * c + 32 * h + 16 * h2
                pgrad[b, first : first + 16, 128 * lane : 128 * lane + 128] = fin[c, h, j].astype(F32)
    for b in range(2):
        kgrad[b, 0:8] = kfin[0, b]
        kgrad[b, 8:9] = kfin[1, b, 0:1]

    for copy in own_grad:
        copy.wait()
    for k in (1, 3, 2):
        for side in range(2):
            remote(
                fg_send.at[k, :, sides[side]], fgrad.at[:, channels((x - k + 4) % 4, side)],
                o_send.at[side, k], o_recv.at[side, k], x_peer(k),
            ).wait_recv()
    for cond, copy in sent:
        if cond is None:
            copy.wait_send()
        else:

            @pl.when(cond)
            def _(copy=copy):
                copy.wait_send()


def body(features, pointwise, depthwise, cotangent):
    shape = features.shape
    anywhere = pl.BlockSpec(memory_space=pl.ANY)
    vmem = pl.BlockSpec(memory_space=pltpu.VMEM)
    dma = pltpu.SemaphoreType.DMA
    out, fgrad, pgrad, kgrad = pl.pallas_call(
        kernel,
        out_shape=(
            jax.ShapeDtypeStruct((CELLS, 2 * CO), BF16),
            jax.ShapeDtypeStruct((CELLS, C), BF16),
            jax.ShapeDtypeStruct((2, LANES, CO), F32),
            jax.ShapeDtypeStruct((2, 9, LANES), F32),
        ),
        in_specs=[anywhere, anywhere, anywhere, vmem],
        out_specs=(vmem, anywhere, vmem, vmem),
        scratch_shapes=[
            pltpu.VMEM((4, CELLS, PART), BF16),
            pltpu.VMEM((4, CELLS, PART), F32),
            pltpu.VMEM((4, 2, 112, PART), F32),
            pltpu.VMEM((4, 2, 9, LANES), BF16),
            pltpu.VMEM((2, 4, CELLS, PART), BF16),
            pltpu.VMEM((2, 4, 2, 64, CO), BF16),
            pltpu.VMEM((2, 16, CO), BF16),
            pltpu.VMEM((2, 9, LANES), BF16),
            pltpu.VMEM((CELLS, 2 * CO), F32),
            pltpu.VMEM((4, CELLS, 2 * CO), BF16),
            pltpu.VMEM((4, CELLS, 2 * CO), BF16),
            pltpu.VMEM((4, CELLS, 2 * CO), BF16),
            pltpu.VMEM((4, CELLS, PART), F32),
            pltpu.VMEM((4, 2, 112, PART), F32),
            pltpu.VMEM((4, CELLS, PART), F32),
            pltpu.VMEM((4, CELLS, PART), BF16),
            pltpu.VMEM((2, 4, 2, 64, CO), F32),
            pltpu.VMEM((2, 4, 2, 64, CO), BF16),
            pltpu.VMEM((4, 2, 64, CO), BF16),
            pltpu.VMEM((8, 2, 32, CO), BF16),
            pltpu.VMEM((8, 2, 32, CO), BF16),
            pltpu.VMEM((8, 16, LANES), BF16),
            pltpu.VMEM((12, 16, LANES), BF16),
            pltpu.VMEM((16, LANES), BF16),
            pltpu.VMEM((2, 4, 2, 8, LANES), F32),
            pltpu.VMEM((4, 2, 8, LANES), F32),
            pltpu.VMEM((8, 8, LANES), F32),
            pltpu.VMEM((8, 8, LANES), F32),
            pltpu.VMEM((8, LANES), F32),
            pltpu.VMEM((12, 8, LANES), F32),
            pltpu.VMEM((8, LANES), F32),
            pltpu.VMEM((2, 2, 8, 16, LANES), BF16),
            pltpu.VMEM((2, 2, 8, LANES), F32),
            dma((2, 4)), dma((2, 4)), dma((2,)),
            dma((2,)), dma((2,)),
            dma((16,)), dma(()),
            dma((16,)), dma((4,)),
            dma(()), dma(()),
            dma((4,)), dma((4,)),
            dma((4,)), dma((4,)),
            dma((2, 4)), dma((2, 4)),
            dma(()), dma(()),
            dma((8,)), dma((8,)),
            dma((8,)), dma(()),
            dma((24,)), dma(()),
            dma(()), dma(()),
            dma(()), dma(()),
            dma((8,)), dma((8,)),
            dma(()), dma(()),
            dma((24,)), dma(()),
            dma(()), dma(()),
        ],
        compiler_params=pltpu.CompilerParams(
            collective_id=0, has_side_effects=True, vmem_limit_bytes=40 * 1024 * 1024
        ),
    )(
        features.reshape(CELLS, C), pointwise, depthwise, cotangent.reshape(CELLS, 2 * CO)
    )
    return (
        out.reshape(*shape[:3], 2 * CO), fgrad.reshape(shape), pgrad, kgrad
    )


def solution(mesh):
    return jax.shard_map(
        body,
        mesh=mesh,
        in_specs=(
            P("dp", "space", None, None),
            P(None, "dp", None),
            P(None, None, "dp"),
            P("dp", "space", None, None),
        ),
        out_specs=(
            P("dp", "space", None, None),
            P("dp", "space", None, None),
            P(None, "dp", None),
            P(None, None, "dp"),
        ),
        check_vma=False,
    )
```

time: 918 us -> 91.4 us (0.10); the launches traced: 908 us -> 90.7 us
  waiting for transfers between devices: 517 us -> 0 us
  blocking collectives: 323 us -> 0 us
  Pallas kernels: 0 us -> 83.7 us
  starting transfers between devices: 23.5 us -> 0 us
  other arithmetic: 14 us -> 0 us
  between operations: 14.4 us -> 0.64 us
    psum x1 -> x0, blocking collectives: 270 us -> none  [body(): sum_w, sum_k = lax.psum((shard_w, shard_k), 'space')]
    reduce_scatter x1 -> x0, waiting for transfers between devices: 243 us -> none  [body(): lax.psum_scatter(part_w.astype(jnp.bfloat16), 'dp', scatter_dimension=1,...]
    unnamed x4 -> x0, waiting for transfers between devices: 212 us -> none
    pallas_call x0 -> x1, Pallas kernels: none -> 83.7 us  [body(): pl.pallas_call(kernel, out_shape=(jax.ShapeDtypeStruct((CELLS, 2 * CO), B...]
    all_gather x1 -> x0, waiting for transfers between devices: 63 us -> none  [body(): lax.all_gather(pointwise, 'dp', axis=1, tiled=True)]
    all_gather x1 -> x0, blocking collectives: 52.7 us -> none  [body(): lax.all_gather(depthwise, 'dp', axis=2, tiled=True)]
    ppermute x8 -> x0, starting transfers between devices: 23.4 us -> none  [shifted(): lax.ppermute(value, axis, [(source, source + steps) for source in range(f...]
  transfers between devices with their start and end apart: 11 -> 0, of which waited for: 3 -> 0; matrix products, arithmetic and copies ran while one was open for 2% -> 0% of each run, Pallas kernels for 0% -> 0%
where the time goes in v1:
time: 91.4 us; the launch traced here: 90.7 us
  Pallas kernels  83.7 us (92%)
  local copies, waits for them, and re-layouts  6.35 us (7%)
    pallas_call x1, Pallas kernels, body(): pl.pallas_call(kernel, out_shape=(jax.ShapeDtypeStruct((CELLS, 2 * CO), B...  83.7 us
    unnamed x11, local copies, waits for them, and re-layouts  6.35 us

profile of v1, /device:TPU:57, one launch (start us, length us, event | category | flops | bytes accessed | tf_op | source)
XLA Modules:
  0.0 90.7 jit_solution(15713351495617862920)
XLA Ops:
  0.6 0.7 copy.8.kin
  1.3 0.0 copy-start
  1.3 1.1 %copy-done = bf16[2,1,72,2048]{3,2,1,0:T(8,128)(2,1)S(1)} copy-done((bf16[2,1,72,2048]{3,2,1,0:T(8,128)(2,1)S(1)}, bf16[2,1,72,2048]{3,2,1,0:T(8,128)(2,1)}, u32[]{:S(2)}) %copy-start) | copy-done | bytes 589848
  2.4 0.0 copy-start.1
  2.4 0.9 %copy-done.1 = bf16[2,1,72,512]{3,2,1,0:T(8,128)(2,1)S(1)} copy-done((bf16[2,1,72,512]{3,2,1,0:T(8,128)(2,1)S(1)}, bf16[2,1,72,512]{3,2,1,0:T(8,128)(2,1)}, u32[]{:S(2)}) %copy-start.1) | copy-done | bytes 147480
  3.3 0.0 copy-start.2
  3.3 0.9 copy-done.2
  4.2 83.7 %shard_map.75 = (bf16[144,512]{1,0:T(8,128)(2,1)S(1)}, bf16[144,2048]{1,0:T(8,128)(2,1)S(1)}, f32[2,128,256]{2,1,0:T(8,128)S(1)}, f32[2,9,128]{2,1,0:T(8,128)S(1)}) custom-call(bf16[144,2048]{1,0:T(8,128)(2,1)S(1)} %bitcast.9, bf16[2,128,256]{2,1,0:T(8,128)(2,1)S(1)} %copy-done.2, bf16[2,9,128]{2,1,0:T(8,128)(2,1)S(1)} %copy.8.kin, bf16[144,512]{1,0:T(8,128)(2,1)S(1)} %bitcast.11), custom_call_target="tpu_custom_call" | custom-call | tf_op jit(solution)/shard_map/pallas_call | solution.py:543
  87.9 0.6 copy.11
  88.5 0.7 copy.15
  89.2 0.8 copy.16
  90.0 0.7 copy.17
Async XLA Ops:
  1.3 1.1 %copy-start = (bf16[2,1,72,2048]{3,2,1,0:T(8,128)(2,1)S(1)}, bf16[2,1,72,2048]{3,2,1,0:T(8,128)(2,1)}, u32[]{:S(2)}) copy-start(bf16[2,1,72,2048]{3,2,1,0:T(8,128)(2,1)} %param.4) | copy-start | bytes 1769476
  2.4 0.9 %copy-start.1 = (bf16[2,1,72,512]{3,2,1,0:T(8,128)(2,1)S(1)}, bf16[2,1,72,512]{3,2,1,0:T(8,128)(2,1)}, u32[]{:S(2)}) copy-start(bf16[2,1,72,512]{3,2,1,0:T(8,128)(2,1)} %param.7) | copy-start | bytes 442372
  3.3 0.9 copy-start.2

commit v2 on v1

--- a/solution.py
+++ b/solution.py
@@ -74,6 +74,16 @@
 
         sent.append((cond, copy))
 
+    def finish():
+        for cond, copy in sent:
+            if cond is None:
+                copy.wait_send()
+            else:
+
+                @pl.when(cond)
+                def _(copy=copy):
+                    copy.wait_send()
+
     def x_peer(k):
         return device_at((x + k) % 4, zl, core, zh, y)
 
@@ -122,8 +132,8 @@
     kg[...] = jnp.zeros_like(kg)
     pl.semaphore_wait(barrier, count - 2 * at_home.astype(jnp.int32))
 
-    for k in (2, 1, 3):
-        for side in range(2):
+    for side in range(2):
+        for k in (2, 1, 3):
             send(
                 feat.at[:, channels((x + k) % 4, side)], rows.at[x, :, sides[side]],
                 f_send.at[side, k], f_recv.at[side, k], x_peer(k),
@@ -138,9 +148,9 @@
         copy.start()
 
     piece = pl.ds(pl.multiple_of(core * 64 + x * 16, 16), 16)
-    antipode = device_at(x, zl, core, 1 - zh, y)
-    send(kin, away_k, a_send.at[0], a_recv.at[0], antipode)
-    send(pw.at[:, piece, :], away_w, a_send.at[1], a_recv.at[1], antipode)
+    partner = device_at(x, (zl + 3) % 6, core, 1 - zh, y)
+    send(kin, away_k, a_send.at[0], a_recv.at[0], partner)
+    send(pw.at[:, piece, :], away_w, a_send.at[1], a_recv.at[1], partner)
     near_slot = zh * 2 + y % 2
     far_slot = (1 - zh) * 2 + y % 2
     not_home = jnp.logical_not(at_home)
@@ -174,35 +184,31 @@
 
     spread_taps(kin, near_slot, 0)
     spread_weights(pw.at[:, piece, :], near_slot, 0)
-    remote(kin, away_k, a_send.at[0], a_recv.at[0], antipode).wait_recv()
+    remote(kin, away_k, a_send.at[0], a_recv.at[0], partner).wait_recv()
     spread_taps(away_k, far_slot, 8)
-    remote(pw.at[:, piece, :], away_w, a_send.at[1], a_recv.at[1], antipode).wait_recv()
+    remote(pw.at[:, piece, :], away_w, a_send.at[1], a_recv.at[1], partner).wait_recv()
     spread_weights(away_w, far_slot, 8)
 
-    for copy in own_rows:
-        copy.wait()
-    for k in (1, 3, 2):
-        for side in range(2):
-            remote(
-                rows.at[x, :, sides[side]], rows.at[(x - k + 4) % 4, :, sides[side]],
-                f_send.at[side, k], f_recv.at[side, k], x_peer(k),
-            ).wait_recv()
-    for slot in range(4):
-        local_wait(taps.at[slot], k_recv.at[slot])
-
-    def stencils(tile):
-        lanes = pl.ds(pl.multiple_of(tile * LANES, LANES), LANES)
+    def tap_of(tile):
+        weights = taps[tile].astype(F32)
+
+        def tap(b, u, v):
+            t = (u + 1) * 3 + v + 1
+            return weights[t, b : b + 1]
+
+        return tap
+
+    def lanes_of(tile):
+        return pl.ds(pl.multiple_of(tile * LANES, LANES), LANES)
+
+    def stencils_a(tile):
+        lanes = lanes_of(tile)
         for r in range(4):
             value = rows[r, :, lanes].astype(F32)
             wide[r, :, lanes] = value
             for i in range(2):
                 moved[r, i, 20:92, lanes] = value[72 * i : 72 * i + 72]
-        weights = taps[tile].astype(F32)
-
-        def tap(b, u, v):
-            t = (u + 1) * 3 + v + 1
-            return weights[b, t : t + 1]
-
+        tap = tap_of(tile)
         for r in range(4):
             pieces = []
             for i in range(2):
@@ -219,6 +225,11 @@
                         total = term if total is None else total + term
                     pieces.append(total)
             dcv[0, r, :, lanes] = jnp.concatenate(pieces, axis=0).astype(BF16)
+
+    def stencils_b(tile):
+        lanes = lanes_of(tile)
+        tap = tap_of(tile)
+        for r in range(4):
             pieces = []
             for i in range(2):
                 for q in range(3):
@@ -235,69 +246,80 @@
                     pieces.append(total)
             dcv[1, r, :, lanes] = jnp.concatenate(pieces, axis=0).astype(BF16)
 
-    pl.loop(0, 2)(stencils)
+    for slot in range(4):
+        local_wait(taps.at[slot], k_recv.at[slot])
+    for side in range(2):
+        own_rows[side].wait()
+        for k in (1, 3, 2):
+            remote(
+                rows.at[x, :, sides[side]], rows.at[(x - k + 4) % 4, :, sides[side]],
+                f_send.at[side, k], f_recv.at[side, k], x_peer(k),
+            ).wait_recv()
+        pl.loop(2 * side, 2 * side + 2)(stencils_a)
+
     local_wait(wts.at[:, :, core], w_recv)
     send(wts.at[:, :, core], wts.at[:, :, core], wc_send, wc_recv, mate)
-    pl.loop(2, 4)(stencils)
+    pl.loop(0, 2)(stencils_b)
     remote(
         wts.at[:, :, core], wts.at[:, :, 1 - core], wc_send, wc_recv, mate
     ).wait_recv()
 
-    for k in (2, 1, 3, 0):
-        r = (x + k) % 4
-        for b in range(2):
+    def products(b):
+        for k in (2, 1, 3, 0):
             part = jnp.dot(
-                dcv[b, r], wts[b].reshape(PART, CO), preferred_element_type=F32
+                dcv[b, (x + k) % 4], wts[b].reshape(PART, CO), preferred_element_type=F32
             )
             if k:
-                send_pre[k, :, b * CO : (b + 1) * CO] = part.astype(BF16)
+                send_pre[b, k] = part.astype(BF16)
+                send(send_pre.at[b, k], got_pre.at[b, k], p_send.at[b, k], p_recv.at[b, k], x_peer(k))
             else:
-                own_pre[:, b * CO : (b + 1) * CO] = part
-        if k:
-            send(send_pre.at[k], got_pre.at[k], p_send.at[k], p_recv.at[k], x_peer(k))
-    for k in (1, 3, 2):
-        remote(send_pre.at[k], got_pre.at[k], p_send.at[k], p_recv.at[k], x_peer(k)).wait_recv()
+                own_pre[b] = part
+
+    products(0)
+    pl.loop(2, 4)(stencils_b)
+    products(1)
     for b in range(2):
         cols = slice(b * CO, (b + 1) * CO)
-        pre = own_pre[:, cols]
         for k in (1, 3, 2):
-            pre = pre + got_pre[k, :, cols].astype(F32)
+            remote(
+                send_pre.at[b, k], got_pre.at[b, k], p_send.at[b, k], p_recv.at[b, k], x_peer(k)
+            ).wait_recv()
+        pre = own_pre[b]
+        for k in (1, 3, 2):
+            pre = pre + got_pre[b, k].astype(F32)
         sig = 1.0 / (1.0 + jnp.exp(-pre))
-        gpre[x, :, cols] = (
-            cot[:, cols].astype(F32) * sig * (1.0 + pre * (1.0 - sig))
-        ).astype(BF16)
+        gpre[b, x] = (cot[:, cols].astype(F32) * sig * (1.0 + pre * (1.0 - sig))).astype(BF16)
+        for k in (2, 1, 3):
+            send(gpre.at[b, x], gpre.at[b, x], g_send.at[b, k], g_recv.at[b, k], x_peer(k))
         out[:, cols] = (pre * sig).astype(BF16)
-    for k in (2, 1, 3):
-        send(gpre.at[x], gpre.at[x], g_send.at[k], g_recv.at[k], x_peer(k))
-    for k in (1, 3, 2):
-        remote(
-            gpre.at[x], gpre.at[(x - k + 4) % 4], g_send.at[k], g_recv.at[k], x_peer(k)
-        ).wait_recv()
-
-    @pl.loop(0, 4)
-    def _(tile):
-        lanes = pl.ds(pl.multiple_of(tile * LANES, LANES), LANES)
-        for b in range(2):
+
+    def wait_gpre(b):
+        for k in (1, 3, 2):
+            remote(
+                gpre.at[b, x], gpre.at[b, (x - k + 4) % 4], g_send.at[b, k], g_recv.at[b, k], x_peer(k)
+            ).wait_recv()
+
+    def weight_gradient(b):
+        @pl.loop(0, 4)
+        def _(tile):
             grad = lax.dot_general(
-                dcv[b, :, :, lanes].reshape(4 * CELLS, LANES),
-                gpre[:, :, b * CO : (b + 1) * CO].reshape(4 * CELLS, CO),
+                dcv[b, :, :, lanes_of(tile)].reshape(4 * CELLS, LANES),
+                gpre[b].reshape(4 * CELLS, CO),
                 (((0,), (0,)), ((), ())),
                 preferred_element_type=F32,
             )
             for half in range(2):
                 block = grad[64 * half : 64 * half + 64]
-                wg_wide[half, tile, b] = block
-                wg[half, tile, b] = block.astype(BF16)
-
-    send(wg.at[1 - core], wg_core, c_send, c_recv, mate)
-
-    @pl.loop(0, 4)
-    def _(r):
-        for b in range(2):
+                wg_wide[b, half, tile] = block
+                wg[b, half, tile] = block.astype(BF16)
+
+        send(wg.at[b, 1 - core], wg_core.at[b], c_send.at[b], c_recv.at[b], mate)
+
+    def stencil_gradient(b):
+        @pl.loop(0, 4)
+        def _(r):
             back = lax.dot_general(
-                gpre[r, :, b * CO : (b + 1) * CO],
-                wts[b].reshape(PART, CO),
-                (((1,), (1,)), ((), ())),
+                gpre[b, r], wts[b].reshape(PART, CO), (((1,), (1,)), ((), ())),
                 preferred_element_type=F32,
             )
             if b:
@@ -307,26 +329,29 @@
                 for i in range(2):
                     ga_moved[r, i, 20:92] = back[72 * i : 72 * i + 72]
 
-    remote(wg.at[1 - core], wg_core, c_send, c_recv, mate).wait_recv()
-    for k in range(8):
-        to = (y + k) % 8
-        slot = to // 2
-        part = pl.ds(pl.multiple_of((to % 2) * 32, 32), 32)
-        for b in range(2):
-            wg_y[k, b] = (
-                wg_wide[core, slot, b, part] + wg_core[slot, b, part].astype(F32)
+    def sum_over_y(b):
+        remote(
+            wg.at[b, 1 - core], wg_core.at[b], c_send.at[b], c_recv.at[b], mate
+        ).wait_recv()
+        for k in (4, 3, 5, 2, 6, 1, 7, 0):
+            to = (y + k) % 8
+            slot = to // 2
+            part = pl.ds(pl.multiple_of((to % 2) * 32, 32), 32)
+            wg_y[b, k] = (
+                wg_wide[b, core, slot, part] + wg_core[b, slot, part].astype(F32)
             ).astype(BF16)
-        if k:
-            send(
-                wg_y.at[k], wg_y_got.at[k], y_send.at[k], y_recv.at[k],
-                device_at(x, zl, core, zh, to),
-            )
-
-    @pl.loop(0, 4)
-    def _(tile):
-        lanes = pl.ds(pl.multiple_of(tile * LANES, LANES), LANES)
-        for b in range(2):
-            step = b + 1
+            if k:
+                send(
+                    wg_y.at[b, k], wg_y_got.at[b, k], y_send.at[b, k], y_recv.at[b, k],
+                    device_at(x, zl, core, zh, to),
+                )
+
+    def tap_gradient(b):
+        step = b + 1
+
+        @pl.loop(0, 4)
+        def _(tile):
+            lanes = lanes_of(tile)
             for u in (-1, 0, 1):
                 sums = [None, None, None]
                 for r in range(4):
@@ -358,16 +383,21 @@
                     total = jnp.sum(sums[v + 1], axis=0, keepdims=True)
                     kg[t // 8, tile, b, t % 8 : t % 8 + 1] = total
 
+    wait_gpre(0)
+    weight_gradient(0)
+    stencil_gradient(0)
+    sum_over_y(0)
+    tap_gradient(0)
+    wait_gpre(1)
+    weight_gradient(1)
+    stencil_gradient(1)
+    sum_over_y(1)
+    tap_gradient(1)
     send(kg.at[1 - core], kg_core, kc_send, kc_recv, mate)
 
     def gradient(tile):
-        lanes = pl.ds(pl.multiple_of(tile * LANES, LANES), LANES)
-        weights = taps[tile].astype(F32)
-
-        def tap(b, u, v):
-            t = (u + 1) * 3 + v + 1
-            return weights[b, t : t + 1]
-
+        lanes = lanes_of(tile)
+        tap = tap_of(tile)
         for r in range(4):
             pieces = []
             for i in range(2):
@@ -401,9 +431,26 @@
                 kg_y.at[k], kg_y_got.at[k], ky_send.at[k], ky_recv.at[k],
                 device_at(x, zl, core, zh, to),
             )
+    home_z = y // 4
+    home_y = 2 * x + (y // 2) % 2
+    for b in range(2):
+        for k in range(1, 8):
+            remote(
+                wg_y.at[b, k], wg_y_got.at[b, k], y_send.at[b, k], y_recv.at[b, k], mate
+            ).wait_recv()
+        total = wg_y[b, 0].astype(F32)
+        for k in range(1, 8):
+            total = total + wg_y_got[b, k].astype(F32)
+        for h in range(2):
+            wg_z[2 * b + h] = total[16 * h : 16 * h + 16].astype(BF16)
+            send_if(
+                jnp.logical_or(zl != 1 + 2 * b + h, zh != home_z),
+                wg_z.at[2 * b + h], wg_z_got.at[z], z_send.at[2 * b + h], z_recv,
+                device_at(x, 1 + 2 * b + h, core, home_z, y),
+            )
     pl.loop(2, 4)(gradient)
-    for k in (2, 1, 3):
-        for side in range(2):
+    for side in range(2):
+        for k in (2, 1, 3):
             send(
                 fg_send.at[(x + k) % 4, :, sides[side]], fgrad.at[:, channels(x, side)],
                 o_send.at[side, k], o_recv.at[side, k], x_peer(k),
@@ -416,26 +463,6 @@
     ]
     for copy in own_grad:
         copy.start()
-
-    for k in range(1, 8):
-        remote(
-            wg_y.at[k], wg_y_got.at[k], y_send.at[k], y_recv.at[k], mate
-        ).wait_recv()
-    for b in range(2):
-        total = wg_y[0, b].astype(F32)
-        for k in range(1, 8):
-            total = total + wg_y_got[k, b].astype(F32)
-        for h in range(2):
-            for lane in range(2):
-                wg_z[b * 4 + h * 2 + lane] = total[
-                    16 * h : 16 * h + 16, 128 * lane : 128 * lane + 128
-                ].astype(BF16)
-    for j in range(8):
-        owner = j if j < 4 else j + 2
-        send_if(
-            z != owner, wg_z.at[j], wg_z_got.at[z], z_send.at[j], z_recv,
-            device_at(x, owner % 6, core, owner // 6, y),
-        )
     for k in range(1, 8):
         remote(
             kg_y.at[k], kg_y_got.at[k], ky_send.at[k], ky_recv.at[k], mate
@@ -445,12 +472,11 @@
         total = total + kg_y_got[k]
     kg_z[...] = total
     send_if(
-        z != 4, kg_z, kg_z_got.at[z], kz_send, kz_recv, device_at(x, 4, core, 0, y)
+        jnp.logical_or(zl != 5, zh != home_z),
+        kg_z, kg_z_got.at[z], kz_send, kz_recv, device_at(x, 5, core, home_z, y),
     )
 
     half = y % 2
-    home_z = y // 4
-    home_y = 2 * x + (y // 2) % 2
     back_sent = []
 
     def spread_sums(src, dst, send_sems, recv_sem):
@@ -481,17 +507,17 @@
 
         back_sent.clear()
 
-    @pl.when(zl < 4)
+    @pl.when((zh == home_z) & (zl > 0) & (zl < 5))
     def _():
         local_wait(wg_z_got, z_recv)
         total = wg_z_got[0].astype(F32)
         for n in range(1, 12):
             total = total + wg_z_got[n].astype(F32)
         wg_red[...] = (total * FACTOR).astype(BF16)
-        spread_sums(wg_red, fin.at[core, half, zh * 4 + zl], b_send, b_recv)
+        spread_sums(wg_red, fin.at[core, half, zl - 1], b_send, b_recv)
         wait_sums()
 
-    @pl.when(z == 4)
+    @pl.when((zh == home_z) & (zl == 5))
     def _():
         local_wait(kg_z_got, kz_recv)
         total = kg_z_got[0]
@@ -509,13 +535,12 @@
     remote(kfin.at[core], kfin.at[1 - core], ke_send, ke_recv, mate).wait_recv()
     for c in range(2):
         for h in range(2):
-            for j in range(8):
-                b, h2, lane = j // 4, (j // 2) % 2, j % 2
-                first = 64 * c + 32 * h + 16 * h2
-                pgrad[b, first : first + 16, 128 * lane : 128 * lane + 128] = fin[c, h, j].astype(F32)
+            for j in range(4):
+                first = 64 * c + 32 * h + 16 * (j % 2)
+                pgrad[j // 2, first : first + 16] = fin[c, h, j].astype(F32)
     for b in range(2):
-        kgrad[b, 0:8] = kfin[0, b]
-        kgrad[b, 8:9] = kfin[1, b, 0:1]
+        for t in range(9):
+            kgrad[t, b : b + 1] = kfin[t // 8, b, t % 8 : t % 8 + 1]
 
     for copy in own_grad:
         copy.wait()
@@ -525,14 +550,19 @@
                 fg_send.at[k, :, sides[side]], fgrad.at[:, channels((x - k + 4) % 4, side)],
                 o_send.at[side, k], o_recv.at[side, k], x_peer(k),
             ).wait_recv()
-    for cond, copy in sent:
-        if cond is None:
-            copy.wait_send()
-        else:
-
-            @pl.when(cond)
-            def _(copy=copy):
-                copy.wait_send()
+    finish()
+
+
+def hand_over(*refs):
+    arrays, results, sems = refs[:4], refs[4:8], refs[8]
+    copies = [
+        pltpu.make_async_copy(array, result, sems.at[n])
+        for n, (array, result) in enumerate(zip(arrays, results))
+    ]
+    for copy in copies:
+        copy.start()
+    for copy in copies:
+        copy.wait()
 
 
 def body(features, pointwise, depthwise, cotangent):
@@ -543,38 +573,38 @@
     out, fgrad, pgrad, kgrad = pl.pallas_call(
         kernel,
         out_shape=(
-            jax.ShapeDtypeStruct((CELLS, 2 * CO), BF16),
-            jax.ShapeDtypeStruct((CELLS, C), BF16),
-            jax.ShapeDtypeStruct((2, LANES, CO), F32),
-            jax.ShapeDtypeStruct((2, 9, LANES), F32),
+            pltpu.VMEM((CELLS, 2 * CO), BF16),
+            pltpu.VMEM((CELLS, C), BF16),
+            pltpu.VMEM((2, LANES, CO), F32),
+            pltpu.VMEM((9, 2, LANES), F32),
         ),
         in_specs=[anywhere, anywhere, anywhere, vmem],
-        out_specs=(vmem, anywhere, vmem, vmem),
+        out_specs=(vmem, vmem, vmem, vmem),
         scratch_shapes=[
             pltpu.VMEM((4, CELLS, PART), BF16),
             pltpu.VMEM((4, CELLS, PART), F32),
             pltpu.VMEM((4, 2, 112, PART), F32),
-            pltpu.VMEM((4, 2, 9, LANES), BF16),
+            pltpu.VMEM((4, 9, 2, LANES), BF16),
             pltpu.VMEM((2, 4, CELLS, PART), BF16),
             pltpu.VMEM((2, 4, 2, 64, CO), BF16),
             pltpu.VMEM((2, 16, CO), BF16),
-            pltpu.VMEM((2, 9, LANES), BF16),
-            pltpu.VMEM((CELLS, 2 * CO), F32),
-            pltpu.VMEM((4, CELLS, 2 * CO), BF16),
-            pltpu.VMEM((4, CELLS, 2 * CO), BF16),
-            pltpu.VMEM((4, CELLS, 2 * CO), BF16),
+            pltpu.VMEM((9, 2, LANES), BF16),
+            pltpu.VMEM((2, CELLS, CO), F32),
+            pltpu.VMEM((2, 4, CELLS, CO), BF16),
+            pltpu.VMEM((2, 4, CELLS, CO), BF16),
+            pltpu.VMEM((2, 4, CELLS, CO), BF16),
             pltpu.VMEM((4, CELLS, PART), F32),
             pltpu.VMEM((4, 2, 112, PART), F32),
             pltpu.VMEM((4, CELLS, PART), F32),
             pltpu.VMEM((4, CELLS, PART), BF16),
-            pltpu.VMEM((2, 4, 2, 64, CO), F32),
-            pltpu.VMEM((2, 4, 2, 64, CO), BF16),
-            pltpu.VMEM((4, 2, 64, CO), BF16),
-            pltpu.VMEM((8, 2, 32, CO), BF16),
-            pltpu.VMEM((8, 2, 32, CO), BF16),
-            pltpu.VMEM((8, 16, LANES), BF16),
-            pltpu.VMEM((12, 16, LANES), BF16),
-            pltpu.VMEM((16, LANES), BF16),
+            pltpu.VMEM((2, 2, 4, 64, CO), F32),
+            pltpu.VMEM((2, 2, 4, 64, CO), BF16),
+            pltpu.VMEM((2, 4, 64, CO), BF16),
+            pltpu.VMEM((2, 8, 32, CO), BF16),
+            pltpu.VMEM((2, 8, 32, CO), BF16),
+            pltpu.VMEM((4, 16, CO), BF16),
+            pltpu.VMEM((12, 16, CO), BF16),
+            pltpu.VMEM((16, CO), BF16),
             pltpu.VMEM((2, 4, 2, 8, LANES), F32),
             pltpu.VMEM((4, 2, 8, LANES), F32),
             pltpu.VMEM((8, 8, LANES), F32),
@@ -582,19 +612,19 @@
             pltpu.VMEM((8, LANES), F32),
             pltpu.VMEM((12, 8, LANES), F32),
             pltpu.VMEM((8, LANES), F32),
-            pltpu.VMEM((2, 2, 8, 16, LANES), BF16),
+            pltpu.VMEM((2, 2, 4, 16, CO), BF16),
             pltpu.VMEM((2, 2, 8, LANES), F32),
             dma((2, 4)), dma((2, 4)), dma((2,)),
             dma((2,)), dma((2,)),
             dma((16,)), dma(()),
             dma((16,)), dma((4,)),
             dma(()), dma(()),
-            dma((4,)), dma((4,)),
-            dma((4,)), dma((4,)),
             dma((2, 4)), dma((2, 4)),
-            dma(()), dma(()),
-            dma((8,)), dma((8,)),
-            dma((8,)), dma(()),
+            dma((2, 4)), dma((2, 4)),
+            dma((2, 4)), dma((2, 4)),
+            dma((2,)), dma((2,)),
+            dma((2, 8)), dma((2, 8)),
+            dma((4,)), dma(()),
             dma((24,)), dma(()),
             dma(()), dma(()),
             dma(()), dma(()),
@@ -604,13 +634,22 @@
             dma(()), dma(()),
         ],
         compiler_params=pltpu.CompilerParams(
-            collective_id=0, has_side_effects=True, vmem_limit_bytes=40 * 1024 * 1024
+            collective_id=0, has_side_effects=True, vmem_limit_bytes=60 * 1024 * 1024
         ),
     )(
-        features.reshape(CELLS, C), pointwise, depthwise, cotangent.reshape(CELLS, 2 * CO)
+        features.reshape(CELLS, C), pointwise, depthwise.transpose(1, 0, 2), cotangent.reshape(CELLS, 2 * CO)
     )
+    made = (out, fgrad, pgrad, kgrad)
+    out, fgrad, pgrad, kgrad = pl.pallas_call(
+        hand_over,
+        out_shape=tuple(jax.ShapeDtypeStruct(m.shape, m.dtype) for m in made),
+        in_specs=[anywhere] * 4,
+        out_specs=(anywhere,) * 4,
+        scratch_shapes=[dma((4,))],
+        compiler_params=pltpu.CompilerParams(vmem_limit_bytes=1024 * 1024),
+    )(*made)
     return (
-        out.reshape(*shape[:3], 2 * CO), fgrad.reshape(shape), pgrad, kgrad
+        out.reshape(*shape[:3], 2 * CO), fgrad.reshape(shape), pgrad, kgrad.transpose(1, 0, 2)
     )
 
 

time: 91.4 us -> 78.1 us (0.85)
  Pallas kernels: 83.7 us -> 77.3 us
  local copies, waits for them, and re-layouts: 6.35 us -> 0 us
    pallas_call x1 -> x2, Pallas kernels: 83.7 us -> 77.3 us  [the longest x1 76.3 us: body(): pl.pallas_call(kernel, out_shape=(pltpu.VMEM((CELLS, 2 * CO), BF16), pltp...]
    unnamed x11 -> x0, local copies, waits for them, and re-layouts: 6.35 us -> none
where the time goes in v2:
time: 78.1 us; the launch traced here: 77.9 us
  Pallas kernels  77.3 us (99%)
    pallas_call x1, Pallas kernels, body(): pl.pallas_call(kernel, out_shape=(pltpu.VMEM((CELLS, 2 * CO), BF16), pltp...  76.3 us

profile of v2, /device:TPU:57, one launch (start us, length us, event | category | flops | bytes accessed | tf_op | source)
XLA Modules:
  0.0 77.9 jit_solution(12115657322127084282)
XLA Ops:
  0.6 76.3 %shard_map.75 = (bf16[144,512]{1,0:T(8,128)(2,1)S(1)}, bf16[144,2048]{1,0:T(8,128)(2,1)S(1)}, f32[2,128,256]{2,1,0:T(8,128)S(1)}, f32[9,2,128]{2,1,0:T(2,128)S(1)}) custom-call(bf16[144,2048]{1,0:T(8,128)(2,1)} %bitcast.10, bf16[2,128,256]{2,1,0:T(8,128)(2,1)} %pw.1, bf16[9,2,128]{2,1,0:T(2,128)(2,1)} %bitcast.12, bf16[144,512]{1,0:T(8,128)(2,1)} %bitcast.11), custom_call_target="tpu_custom_call" | custom-call | tf_op jit(solution)/shard_map/pallas_call | solution.py:573
  77.0 1.0 %shard_map.76 = (bf16[144,512]{1,0:T(8,128)(2,1)}, bf16[144,2048]{1,0:T(8,128)(2,1)}, f32[2,128,256]{2,1,0:T(8,128)}, f32[9,2,128]{2,1,0:T(2,128)}) custom-call(bf16[144,512]{1,0:T(8,128)(2,1)S(1)} %get-tuple-element.12.refs_0_, bf16[144,2048]{1,0:T(8,128)(2,1)S(1)} %get-tuple-element.13.refs_1_, f32[2,128,256]{2,1,0:T(8,128)S(1)} %get-tuple-element.14.refs_2_, ...), custom_call_target="tpu_custom_call" | custom-call | tf_op jit(solution)/shard_map/pallas_call | solution.py:643

commit v3 on v2

--- a/solution.py
+++ b/solution.py
@@ -27,14 +27,14 @@
 def kernel(
     feat, pw, kin, cot,
     out, fgrad, pgrad, kgrad,
-    rows, wide, moved, taps, dcv, wts, away_w, away_k,
+    rows, cot_here, wide, moved, taps, dcv, wts, away_w, away_k,
     own_pre, send_pre, got_pre, gpre, ga, ga_moved, gb, fg_send,
     wg_wide, wg, wg_core, wg_y, wg_y_got, wg_z, wg_z_got, wg_red,
-    kg, kg_core, kg_y, kg_y_got, kg_z, kg_z_got, kg_red, fin, kfin,
-    f_send, f_recv, own_sem, a_send, a_recv, w_send, w_recv, k_send, k_recv, wc_send, wc_recv,
+    kg, kg_got, kg_z, kg_z_got, kg_red, mid, kmid, fin, kfin,
+    f_send, f_recv, own_sem, cot_sem, a_send, a_recv, w_send, w_recv, k_send, k_recv, wc_send, wc_recv,
     p_send, p_recv, g_send, g_recv, o_send, o_recv,
-    c_send, c_recv, y_send, y_recv, z_send, z_recv, b_send, b_recv, e_send, e_recv,
-    kc_send, kc_recv, ky_send, ky_recv, kz_send, kz_recv, kb_send, kb_recv, ke_send, ke_recv,
+    c_send, c_recv, y_send, y_recv, z_send, z_recv, b_send, b_recv, d_send, d_recv, e_send, e_recv,
+    ky_send, ky_recv, kz_send, kz_recv, kb_send, kb_recv, kd_send, kd_recv, ke_send, ke_recv,
 ):
     space = lax.axis_index("space")
     dp = lax.axis_index("dp")
@@ -127,17 +127,55 @@
         greet(device_at(plane, zl, core, zh, y))
 
     count += 9
-    moved[...] = jnp.zeros_like(moved)
-    ga_moved[...] = jnp.zeros_like(ga_moved)
-    kg[...] = jnp.zeros_like(kg)
     pl.semaphore_wait(barrier, count - 2 * at_home.astype(jnp.int32))
 
-    for side in range(2):
+    def send_rows(side):
         for k in (2, 1, 3):
             send(
                 feat.at[:, channels((x + k) % 4, side)], rows.at[x, :, sides[side]],
                 f_send.at[side, k], f_recv.at[side, k], x_peer(k),
             )
+
+    piece = pl.ds(pl.multiple_of(core * 64 + x * 16, 16), 16)
+    partner = device_at(x, (zl + 3) % 6, core, 1 - zh, y)
+    send(kin, away_k, a_send.at[2], a_recv.at[2], partner)
+    for b in range(2):
+        send(pw.at[b, piece], away_w.at[b], a_send.at[b], a_recv.at[b], partner)
+    near_slot = zh * 2 + y % 2
+    far_slot = (1 - zh) * 2 + y % 2
+    not_home = jnp.logical_not(at_home)
+
+    def spread_taps(src, slot, base):
+        for k in range(8):
+            target = device_at(plane, zl, core, zh, (y + k) % 8)
+            if k == 0:
+                here = pltpu.make_async_copy(src, taps.at[slot], k_recv.at[slot])
+
+                @pl.when(at_home)
+                def _(here=here):
+                    here.start()
+            else:
+                copy = remote(src, taps.at[slot], k_send.at[base + k], k_recv.at[slot], target)
+
+                @pl.when(at_home)
+                def _(copy=copy):
+                    copy.start()
+
+                sent.append((at_home, copy))
+
+    def spread_weights(b, src, slot, base):
+        for k in range(8):
+            target = device_at(plane, zl, core, zh, (y + k) % 8)
+            dst = wts.at[b, slot, core, pl.ds(pl.multiple_of(x * 16, 16), 16)]
+            if k == 0:
+                send_if(not_home, src, dst, w_send.at[base], w_recv.at[b], target)
+            else:
+                send(src, dst, w_send.at[base + k], w_recv.at[b], target)
+
+    spread_taps(kin, near_slot, 0)
+    for b in range(2):
+        spread_weights(b, pw.at[b, piece], near_slot, 16 * b)
+    send_rows(0)
     own_rows = [
         pltpu.make_async_copy(
             feat.at[:, channels(x, side)], rows.at[x, :, sides[side]], own_sem.at[side]
@@ -146,48 +184,21 @@
     ]
     for copy in own_rows:
         copy.start()
-
-    piece = pl.ds(pl.multiple_of(core * 64 + x * 16, 16), 16)
-    partner = device_at(x, (zl + 3) % 6, core, 1 - zh, y)
-    send(kin, away_k, a_send.at[0], a_recv.at[0], partner)
-    send(pw.at[:, piece, :], away_w, a_send.at[1], a_recv.at[1], partner)
-    near_slot = zh * 2 + y % 2
-    far_slot = (1 - zh) * 2 + y % 2
-    not_home = jnp.logical_not(at_home)
-
-    def spread_taps(src, slot, base):
-        for k in range(8):
-            target = device_at(plane, zl, core, zh, (y + k) % 8)
-            if k == 0:
-                here = pltpu.make_async_copy(src, taps.at[slot], k_recv.at[slot])
-
-                @pl.when(at_home)
-                def _(here=here):
-                    here.start()
-            else:
-                copy = remote(src, taps.at[slot], k_send.at[base + k], k_recv.at[slot], target)
-
-                @pl.when(at_home)
-                def _(copy=copy):
-                    copy.start()
-
-                sent.append((at_home, copy))
-
-    def spread_weights(src, slot, base):
-        for k in range(8):
-            target = device_at(plane, zl, core, zh, (y + k) % 8)
-            dst = wts.at[:, slot, core, pl.ds(pl.multiple_of(x * 16, 16), 16)]
-            if k == 0:
-                send_if(not_home, src, dst, w_send.at[base], w_recv, target)
-            else:
-                send(src, dst, w_send.at[base + k], w_recv, target)
-
-    spread_taps(kin, near_slot, 0)
-    spread_weights(pw.at[:, piece, :], near_slot, 0)
-    remote(kin, away_k, a_send.at[0], a_recv.at[0], partner).wait_recv()
+    cot_copy = pltpu.make_async_copy(cot, cot_here, cot_sem)
+    cot_copy.start()
+    border = jnp.zeros((24, PART), F32)
+    for r in range(4):
+        for i in range(2):
+            for array in (moved, ga_moved):
+                array[r, i, 0:24] = border
+                array[r, i, 88:112] = border
+    kg[...] = jnp.zeros_like(kg)
+    remote(kin, away_k, a_send.at[2], a_recv.at[2], partner).wait_recv()
     spread_taps(away_k, far_slot, 8)
-    remote(pw.at[:, piece, :], away_w, a_send.at[1], a_recv.at[1], partner).wait_recv()
-    spread_weights(away_w, far_slot, 8)
+    for b in range(2):
+        remote(pw.at[b, piece], away_w.at[b], a_send.at[b], a_recv.at[b], partner).wait_recv()
+        spread_weights(b, away_w.at[b], far_slot, 16 * b + 8)
+    send_rows(1)
 
     def tap_of(tile):
         weights = taps[tile].astype(F32)
@@ -257,12 +268,18 @@
             ).wait_recv()
         pl.loop(2 * side, 2 * side + 2)(stencils_a)
 
-    local_wait(wts.at[:, :, core], w_recv)
-    send(wts.at[:, :, core], wts.at[:, :, core], wc_send, wc_recv, mate)
-    pl.loop(0, 2)(stencils_b)
-    remote(
-        wts.at[:, :, core], wts.at[:, :, 1 - core], wc_send, wc_recv, mate
-    ).wait_recv()
+    def trade_weights(b):
+        local_wait(wts.at[b, :, core], w_recv.at[b])
+        send(wts.at[b, :, core], wts.at[b, :, core], wc_send.at[b], wc_recv.at[b], mate)
+
+    def wait_weights(b):
+        remote(
+            wts.at[b, :, core], wts.at[b, :, 1 - core], wc_send.at[b], wc_recv.at[b], mate
+        ).wait_recv()
+
+    trade_weights(0)
+    pl.loop(0, 4)(stencils_b)
+    trade_weights(1)
 
     def products(b):
         for k in (2, 1, 3, 0):
@@ -275,9 +292,11 @@
             else:
                 own_pre[b] = part
 
+    wait_weights(0)
     products(0)
-    pl.loop(2, 4)(stencils_b)
+    wait_weights(1)
     products(1)
+    cot_copy.wait()
     for b in range(2):
         cols = slice(b * CO, (b + 1) * CO)
         for k in (1, 3, 2):
@@ -288,7 +307,7 @@
         for k in (1, 3, 2):
             pre = pre + got_pre[b, k].astype(F32)
         sig = 1.0 / (1.0 + jnp.exp(-pre))
-        gpre[b, x] = (cot[:, cols].astype(F32) * sig * (1.0 + pre * (1.0 - sig))).astype(BF16)
+        gpre[b, x] = (cot_here[:, cols].astype(F32) * sig * (1.0 + pre * (1.0 - sig))).astype(BF16)
         for k in (2, 1, 3):
             send(gpre.at[b, x], gpre.at[b, x], g_send.at[b, k], g_recv.at[b, k], x_peer(k))
         out[:, cols] = (pre * sig).astype(BF16)
@@ -393,7 +412,15 @@
     stencil_gradient(1)
     sum_over_y(1)
     tap_gradient(1)
-    send(kg.at[1 - core], kg_core, kc_send, kc_recv, mate)
+    for k in (4, 3, 5, 2, 6, 1, 7, 0):
+        to = (y + k) % 8
+        for turn in range(2):
+            to_core = (core + turn) % 2
+            if k or turn:
+                send(
+                    kg.at[to_core, to // 2, to % 2], kg_got.at[k, turn],
+                    ky_send.at[k, turn], ky_recv.at[k, turn], device_at(x, zl, to_core, zh, to),
+                )
 
     def gradient(tile):
         lanes = lanes_of(tile)
@@ -421,19 +448,26 @@
                     pieces.append(total)
             fg_send[r, :, lanes] = jnp.concatenate(pieces, axis=0).astype(BF16)
 
-    pl.loop(0, 2)(gradient)
-    remote(kg.at[1 - core], kg_core, kc_send, kc_recv, mate).wait_recv()
-    for k in range(8):
-        to = (y + k) % 8
-        kg_y[k] = kg[core, to // 2, to % 2] + kg_core[to // 2, to % 2]
-        if k:
+    for side in range(2):
+        pl.loop(2 * side, 2 * side + 2)(gradient)
+        for k in (2, 1, 3):
             send(
-                kg_y.at[k], kg_y_got.at[k], ky_send.at[k], ky_recv.at[k],
-                device_at(x, zl, core, zh, to),
+                fg_send.at[(x + k) % 4, :, sides[side]], fgrad.at[:, channels(x, side)],
+                o_send.at[side, k], o_recv.at[side, k], x_peer(k),
             )
+    own_grad = [
+        pltpu.make_async_copy(
+            fg_send.at[x, :, sides[side]], fgrad.at[:, channels(x, side)], own_sem.at[side]
+        )
+        for side in range(2)
+    ]
+    for copy in own_grad:
+        copy.start()
+
     home_z = y // 4
     home_y = 2 * x + (y // 2) % 2
-    for b in range(2):
+
+    def sum_over_z(b):
         for k in range(1, 8):
             remote(
                 wg_y.at[b, k], wg_y_got.at[b, k], y_send.at[b, k], y_recv.at[b, k], mate
@@ -448,28 +482,17 @@
                 wg_z.at[2 * b + h], wg_z_got.at[z], z_send.at[2 * b + h], z_recv,
                 device_at(x, 1 + 2 * b + h, core, home_z, y),
             )
-    pl.loop(2, 4)(gradient)
-    for side in range(2):
-        for k in (2, 1, 3):
-            send(
-                fg_send.at[(x + k) % 4, :, sides[side]], fgrad.at[:, channels(x, side)],
-                o_send.at[side, k], o_recv.at[side, k], x_peer(k),
-            )
-    own_grad = [
-        pltpu.make_async_copy(
-            fg_send.at[x, :, sides[side]], fgrad.at[:, channels(x, side)], own_sem.at[side]
-        )
-        for side in range(2)
-    ]
-    for copy in own_grad:
-        copy.start()
-    for k in range(1, 8):
-        remote(
-            kg_y.at[k], kg_y_got.at[k], ky_send.at[k], ky_recv.at[k], mate
-        ).wait_recv()
-    total = kg_y[0]
-    for k in range(1, 8):
-        total = total + kg_y_got[k]
+
+    sum_over_z(0)
+    sum_over_z(1)
+    total = kg[core, y // 2, y % 2]
+    for k in range(8):
+        for turn in range(2):
+            if k or turn:
+                remote(
+                    kg.at[0, 0, 0], kg_got.at[k, turn], ky_send.at[k, turn], ky_recv.at[k, turn], mate
+                ).wait_recv()
+                total = total + kg_got[k, turn]
     kg_z[...] = total
     send_if(
         jnp.logical_or(zl != 5, zh != home_z),
@@ -477,70 +500,102 @@
     )
 
     half = y % 2
-    back_sent = []
-
-    def spread_sums(src, dst, send_sems, recv_sem):
-        for n in range(24):
-            to_x, to_z = n // 6, n % 6
-            same = (to_x == x) & (to_z == zl) & (home_z == zh) & (home_y == y)
-            copy = remote(
-                src, dst, send_sems.at[n], recv_sem, device_at(to_x, to_z, core, home_z, home_y)
-            )
-            here = pltpu.make_async_copy(src, dst, recv_sem)
+    sums_weights = (zl > 0) & (zl < 5)
+    sums_taps = zl == 5
+
+    def spread(src, dst, send_sems, recv_sem, targets, start):
+        for n, (same, target) in enumerate(targets):
+            copy = remote(src, dst, send_sems.at[n], recv_sem, target)
 
             @pl.when(jnp.logical_not(same))
             def _(copy=copy):
-                copy.start()
-
-            @pl.when(same)
-            def _(here=here):
-                here.start()
-
-            back_sent.append((same, copy))
-
-    def wait_sums():
-        for same, copy in back_sent:
-
-            @pl.when(jnp.logical_not(same))
-            def _(copy=copy):
-                copy.wait_send()
-
-        back_sent.clear()
-
-    @pl.when((zh == home_z) & (zl > 0) & (zl < 5))
+                copy.start() if start else copy.wait_send()
+
+            if start:
+                here = pltpu.make_async_copy(src, dst, recv_sem)
+
+                @pl.when(same)
+                def _(here=here):
+                    here.start()
+
+    def planes():
+        return [
+            ((x == n) & (home_y == y), device_at(n, zl, core, home_z, home_y)) for n in range(4)
+        ]
+
+    def along_z():
+        return [(zl == n, device_at(x, n, core, zh, y)) for n in range(6)]
+
+    def first(weights, start):
+        if weights:
+            spread(wg_red, mid.at[half], b_send, b_recv, planes(), start)
+        else:
+            spread(kg_red, kmid.at[half], kb_send, kb_recv, planes(), start)
+
+    def second(weights, start):
+        if weights:
+            spread(mid, fin.at[core, zl - 1], d_send, d_recv, along_z(), start)
+        else:
+            spread(kmid, kfin.at[core], kd_send, kd_recv, along_z(), start)
+
+    @pl.when(sums_weights & (zh == home_z))
     def _():
         local_wait(wg_z_got, z_recv)
         total = wg_z_got[0].astype(F32)
         for n in range(1, 12):
             total = total + wg_z_got[n].astype(F32)
         wg_red[...] = (total * FACTOR).astype(BF16)
-        spread_sums(wg_red, fin.at[core, half, zl - 1], b_send, b_recv)
-        wait_sums()
-
-    @pl.when((zh == home_z) & (zl == 5))
+        first(True, True)
+
+    @pl.when(sums_taps & (zh == home_z))
     def _():
         local_wait(kg_z_got, kz_recv)
         total = kg_z_got[0]
         for n in range(1, 12):
             total = total + kg_z_got[n]
         kg_red[...] = total * FACTOR
-        spread_sums(kg_red, kfin.at[core, half], kb_send, kb_recv)
-        wait_sums()
-
-    local_wait(fin.at[core], b_recv)
+        first(False, True)
+
+    @pl.when(sums_weights)
+    def _():
+        local_wait(mid, b_recv)
+        second(True, True)
+
+    @pl.when(sums_taps)
+    def _():
+        local_wait(kmid, kb_recv)
+        second(False, True)
+
+    local_wait(fin.at[core], d_recv)
     send(fin.at[core], fin.at[core], e_send, e_recv, mate)
-    local_wait(kfin.at[core], kb_recv)
+    local_wait(kfin.at[core], kd_recv)
     send(kfin.at[core], kfin.at[core], ke_send, ke_recv, mate)
     remote(fin.at[core], fin.at[1 - core], e_send, e_recv, mate).wait_recv()
     remote(kfin.at[core], kfin.at[1 - core], ke_send, ke_recv, mate).wait_recv()
     for c in range(2):
         for h in range(2):
             for j in range(4):
-                first = 64 * c + 32 * h + 16 * (j % 2)
-                pgrad[j // 2, first : first + 16] = fin[c, h, j].astype(F32)
+                start = 64 * c + 32 * h + 16 * (j % 2)
+                pgrad[j // 2, start : start + 16] = fin[c, j, h].astype(F32)
     for b in range(2):
         for t in range(9):
             kgrad[t, b : b + 1] = kfin[t // 8, b, t % 8 : t % 8 + 1]
+
+    @pl.when(sums_weights & (zh == home_z))
+    def _():
+        first(True, False)
+
+    @pl.when(sums_taps & (zh == home_z))
+    def _():
+        first(False, False)
+
+    @pl.when(sums_weights)
+    def _():
+        second(True, False)
+
+    @pl.when(sums_taps)
+    def _():
+        second(False, False)
 
     for copy in own_grad:
         copy.wait()
@@ -578,10 +633,11 @@
             pltpu.VMEM((2, LANES, CO), F32),
             pltpu.VMEM((9, 2, LANES), F32),
         ),
-        in_specs=[anywhere, anywhere, anywhere, vmem],
+        in_specs=[anywhere] * 4,
         out_specs=(vmem, vmem, vmem, vmem),
         scratch_shapes=[
             pltpu.VMEM((4, CELLS, PART), BF16),
+            pltpu.VMEM((CELLS, 2 * CO), BF16),
             pltpu.VMEM((4, CELLS, PART), F32),
             pltpu.VMEM((4, 2, 112, PART), F32),
             pltpu.VMEM((4, 9, 2, LANES), BF16),
@@ -606,31 +662,32 @@
             pltpu.VMEM((12, 16, CO), BF16),
             pltpu.VMEM((16, CO), BF16),
             pltpu.VMEM((2, 4, 2, 8, LANES), F32),
-            pltpu.VMEM((4, 2, 8, LANES), F32),
-            pltpu.VMEM((8, 8, LANES), F32),
-            pltpu.VMEM((8, 8, LANES), F32),
+            pltpu.VMEM((8, 2, 8, LANES), F32),
             pltpu.VMEM((8, LANES), F32),
             pltpu.VMEM((12, 8, LANES), F32),
             pltpu.VMEM((8, LANES), F32),
-            pltpu.VMEM((2, 2, 4, 16, CO), BF16),
+            pltpu.VMEM((2, 16, CO), BF16),
+            pltpu.VMEM((2, 8, LANES), F32),
+            pltpu.VMEM((2, 4, 2, 16, CO), BF16),
             pltpu.VMEM((2, 2, 8, LANES), F32),
-            dma((2, 4)), dma((2, 4)), dma((2,)),
+            dma((2, 4)), dma((2, 4)), dma((2,)), dma(()),
+            dma((3,)), dma((3,)),
+            dma((32,)), dma((2,)),
+            dma((16,)), dma((4,)),
             dma((2,)), dma((2,)),
-            dma((16,)), dma(()),
-            dma((16,)), dma((4,)),
-            dma(()), dma(()),
             dma((2, 4)), dma((2, 4)),
             dma((2, 4)), dma((2, 4)),
             dma((2, 4)), dma((2, 4)),
             dma((2,)), dma((2,)),
             dma((2, 8)), dma((2, 8)),
             dma((4,)), dma(()),
-            dma((24,)), dma(()),
+            dma((4,)), dma(()),
+            dma((6,)), dma(()),
             dma(()), dma(()),
+            dma((8, 2)), dma((8, 2)),
             dma(()), dma(()),
-            dma((8,)), dma((8,)),
-            dma(()), dma(()),
-            dma((24,)), dma(()),
+            dma((4,)), dma(()),
+            dma((6,)), dma(()),
             dma(()), dma(()),
         ],
         compiler_params=pltpu.CompilerParams(

time: 78.1 us -> 77.2 us (0.988)
  Pallas kernels: 77.3 us -> 76.2 us
    pallas_call x1, Pallas kernels: 76.3 us -> 75.3 us  [body(): pl.pallas_call(kernel, out_shape=(pltpu.VMEM((CELLS, 2 * CO), BF16), pltp...]
where the time goes in v3:
time: 77.2 us; the launch traced here: 76.9 us
  Pallas kernels  76.2 us (99%)
    pallas_call x1, Pallas kernels, body(): pl.pallas_call(kernel, out_shape=(pltpu.VMEM((CELLS, 2 * CO), BF16), pltp...  75.3 us

profile of v3, /device:TPU:57, one launch (start us, length us, event | category | flops | bytes accessed | tf_op | source)
XLA Modules:
  0.0 76.9 jit_solution(10055995184158697767)
XLA Ops:
  0.6 75.3 %shard_map.75 = (bf16[144,512]{1,0:T(8,128)(2,1)S(1)}, bf16[144,2048]{1,0:T(8,128)(2,1)S(1)}, f32[2,128,256]{2,1,0:T(8,128)S(1)}, f32[9,2,128]{2,1,0:T(2,128)S(1)}) custom-call(bf16[144,2048]{1,0:T(8,128)(2,1)} %bitcast.10, bf16[2,128,256]{2,1,0:T(8,128)(2,1)} %pw.1, bf16[9,2,128]{2,1,0:T(2,128)(2,1)} %bitcast.12, bf16[144,512]{1,0:T(8,128)(2,1)} %bitcast.11), custom_call_target="tpu_custom_call" | custom-call | tf_op jit(solution)/shard_map/pallas_call | solution.py:628
  75.9 1.0 %shard_map.76 = (bf16[144,512]{1,0:T(8,128)(2,1)}, bf16[144,2048]{1,0:T(8,128)(2,1)}, f32[2,128,256]{2,1,0:T(8,128)}, f32[9,2,128]{2,1,0:T(2,128)}) custom-call(bf16[144,512]{1,0:T(8,128)(2,1)S(1)} %get-tuple-element.12.refs_0_, bf16[144,2048]{1,0:T(8,128)(2,1)S(1)} %get-tuple-element.13.refs_1_, f32[2,128,256]{2,1,0:T(8,128)S(1)} %get-tuple-element.14.refs_2_, ...), custom_call_target="tpu_custom_call" | custom-call | tf_op jit(solution)/shard_map/pallas_call | solution.py:700

commit v4 on v3

--- a/solution.py
+++ b/solution.py
@@ -406,11 +406,11 @@
     weight_gradient(0)
     stencil_gradient(0)
     sum_over_y(0)
-    tap_gradient(0)
     wait_gpre(1)
     weight_gradient(1)
     stencil_gradient(1)
     sum_over_y(1)
+    tap_gradient(0)
     tap_gradient(1)
     for k in (4, 3, 5, 2, 6, 1, 7, 0):
         to = (y + k) % 8
@@ -570,13 +570,17 @@
     send(fin.at[core], fin.at[core], e_send, e_recv, mate)
     local_wait(kfin.at[core], kd_recv)
     send(kfin.at[core], kfin.at[core], ke_send, ke_recv, mate)
-    remote(fin.at[core], fin.at[1 - core], e_send, e_recv, mate).wait_recv()
-    remote(kfin.at[core], kfin.at[1 - core], ke_send, ke_recv, mate).wait_recv()
-    for c in range(2):
+
+    def place(c):
         for h in range(2):
             for j in range(4):
-                start = 64 * c + 32 * h + 16 * (j % 2)
-                pgrad[j // 2, start : start + 16] = fin[c, j, h].astype(F32)
+                start = pl.multiple_of(64 * c + 32 * h + 16 * (j % 2), 16)
+                pgrad[j // 2, pl.ds(start, 16)] = fin[c, j, h].astype(F32)
+
+    place(core)
+    remote(fin.at[core], fin.at[1 - core], e_send, e_recv, mate).wait_recv()
+    place(1 - core)
+    remote(kfin.at[core], kfin.at[1 - core], ke_send, ke_recv, mate).wait_recv()
     for b in range(2):
         for t in range(9):
             kgrad[t, b : b + 1] = kfin[t // 8, b, t % 8 : t % 8 + 1]

time: 77.2 us -> 76.4 us (0.990)
  no operation moved by 1% of the time
where the time goes in v4:
time: 76.4 us; the launch traced here: 76.3 us
  Pallas kernels  75.6 us (99%)
    pallas_call x1, Pallas kernels, body(): pl.pallas_call(kernel, out_shape=(pltpu.VMEM((CELLS, 2 * CO), BF16), pltp...  74.7 us

profile of v4, /device:TPU:57, one launch (start us, length us, event | category | flops | bytes accessed | tf_op | source)
XLA Modules:
  0.0 76.3 jit_solution(2241387085683987565)
XLA Ops:
  0.6 74.7 %shard_map.75 = (bf16[144,512]{1,0:T(8,128)(2,1)S(1)}, bf16[144,2048]{1,0:T(8,128)(2,1)S(1)}, f32[2,128,256]{2,1,0:T(8,128)S(1)}, f32[9,2,128]{2,1,0:T(2,128)S(1)}) custom-call(bf16[144,2048]{1,0:T(8,128)(2,1)} %bitcast.10, bf16[2,128,256]{2,1,0:T(8,128)(2,1)} %pw.1, bf16[9,2,128]{2,1,0:T(2,128)(2,1)} %bitcast.12, bf16[144,512]{1,0:T(8,128)(2,1)} %bitcast.11), custom_call_target="tpu_custom_call" | custom-call | tf_op jit(solution)/shard_map/pallas_call | solution.py:632
  75.3 1.0 %shard_map.76 = (bf16[144,512]{1,0:T(8,128)(2,1)}, bf16[144,2048]{1,0:T(8,128)(2,1)}, f32[2,128,256]{2,1,0:T(8,128)}, f32[9,2,128]{2,1,0:T(2,128)}) custom-call(bf16[144,512]{1,0:T(8,128)(2,1)S(1)} %get-tuple-element.12.refs_0_, bf16[144,2048]{1,0:T(8,128)(2,1)S(1)} %get-tuple-element.13.refs_1_, f32[2,128,256]{2,1,0:T(8,128)S(1)} %get-tuple-element.14.refs_2_, ...), custom_call_target="tpu_custom_call" | custom-call | tf_op jit(solution)/shard_map/pallas_call | solution.py:704
